TPU v7x, 128 devices: a whole 4x4x4 slice. The times are simulated.
128 devices in a mesh: layer: 2 (over y_hi), row: 8 (over z, core), col: 8 (over y_lo, x).
Axes of the slice: x: 4, y: 4 (y_hi: 2, y_lo: 2; y = y_hi * 2 + y_lo), z: 4, core: 2. Of those that a mesh axis runs over, the one named last changes fastest.
Arguments:
- rhs: bfloat16 [4, 8, 256, 512], P(None, 'row'), may hold values from -6 to 6
- dinv: bfloat16 [4, 8, 512, 512], P(None, 'row'), may hold values from -3 to 3
- factor: bfloat16 [3, 8, 192, 512, 512], P(None, 'row', ('layer', 'col')), may hold values from -0.02734375 to 0.02734375
- deps: int32 [3, 8, 192], P(None, 'row', ('layer', 'col')), may hold values from 0 to 23, as said below
- counts: int32 [3, 8, 16], P(None, 'row', ('layer', 'col')), may hold values from 0 to 12
- sizes: int32 [4, 8], P(None, 'row'), may hold values from 128 to 512
Outputs:
- forward: bfloat16 [4, 8, 256, 512], P(None, 'row')
- solution: bfloat16 [4, 8, 256, 512], P(None, 'row')
Inputs may be any that keep to these rules, and one draw needn't show every extreme that they name: `deps`: a slot of block-row (l, r) at index l - 1 names a block of an earlier level, l2 * 8 + r2 with l2 < l; several slots may name one block.
All inputs are finite; a program needn't handle non-finite values.
Results may differ from a plain program's by a relative error of at most 0.013.
Values may be sent and summed in bfloat16 or wider, within the bound.
A program may use at most 128 MiB of HBM per device.

v0:
```python
import jax
import jax.numpy as jnp
from jax import lax
from jax.sharding import PartitionSpec as P


def live_rows(size, width):
    return (lax.broadcasted_iota(jnp.int32, (1, width), 1) < size).astype(jnp.float32)


def slot_mask(count, slots):
    return (lax.broadcasted_iota(jnp.int32, (slots, 1, 1), 0) < count).astype(jnp.bfloat16)


def solve_forward(resid, inverse, live):
    product = lax.dot_general(
        resid, inverse, (((1,), (1,)), ((), ())), preferred_element_type=jnp.float32
    )
    return (product * live).astype(jnp.bfloat16)


def solve_backward(resid, inverse, live):
    return (jnp.dot(resid, inverse, preferred_element_type=jnp.float32) * live).astype(jnp.bfloat16)


def shards(rhs, dinv, factor, deps, counts, sizes):
    levels = rhs.shape[0]
    rhs_cols = rhs.shape[2]
    width = rhs.shape[3]
    slots = factor.shape[2]
    share = rhs_cols // lax.axis_size(("layer", "col"))
    nbr = lax.axis_size("row")
    mine = lax.axis_index(("layer", "col"))
    forward = []
    stash = []
    for level in range(levels):
        live = live_rows(sizes[level, 0], width)
        inverse = dinv[level, 0]
        if level == 0:
            solved = solve_forward(rhs[0, 0], inverse, live)
        else:
            known = jnp.concatenate(stash, axis=0)
            picked = jnp.take(known, deps[level - 1, 0], axis=0) * slot_mask(
                counts[level - 1, 0, 0], slots
            )
            partial_value = jnp.einsum(
                "kni,kji->nj", picked, factor[level - 1, 0], preferred_element_type=jnp.float32
            )
            total = lax.psum(partial_value, ("layer", "col"))
            solved = solve_forward(
                (rhs[level, 0].astype(jnp.float32) - total).astype(jnp.bfloat16), inverse, live
            )
        forward.append(solved)
        if level + 1 < levels:
            stash.append(lax.all_gather(solved[None], "row", axis=0, tiled=True))
    carried = jnp.zeros((levels * nbr, rhs_cols, width), jnp.float32)
    solution = [None] * levels
    for level in range(levels - 1, -1, -1):
        live = live_rows(sizes[level, 0], width)
        inverse = dinv[level, 0]
        if level == levels - 1:
            solved = solve_backward(forward[level], inverse, live)
        else:
            block = carried[level * nbr : (level + 1) * nbr]
            layers = lax.axis_size("layer")
            arranged = block.reshape(nbr, layers, rhs_cols // layers, width).transpose(1, 0, 2, 3)
            arranged = arranged.reshape(nbr * rhs_cols, width)
            summed = lax.psum_scatter(
                arranged, ("layer", "row", "col"), scatter_dimension=0, tiled=True
            )
            own = lax.dynamic_slice_in_dim(forward[level], mine * share, share, 0)
            piece = solve_backward(
                (own.astype(jnp.float32) - summed).astype(jnp.bfloat16), inverse, live
            )
            solved = lax.all_gather(piece, ("layer", "col"), axis=0, tiled=True)
        solution[level] = solved
        if level > 0:
            terms = jnp.einsum(
                "nj,kji->kni", solved, factor[level - 1, 0], preferred_element_type=jnp.float32
            )
            terms = terms * slot_mask(counts[level - 1, 0, 0], slots).astype(jnp.float32)
            carried = carried.at[deps[level - 1, 0]].add(terms)
    return (jnp.stack(forward)[:, None], jnp.stack(solution)[:, None])


def solution(mesh):
    placed = (
        P(None, "row", None, None),
        P(None, "row", None, None),
        P(None, "row", ("layer", "col"), None, None),
        P(None, "row", ("layer", "col")),
        P(None, "row", ("layer", "col")),
        P(None, "row"),
    )
    return jax.shard_map(
        shards,
        mesh=mesh,
        in_specs=placed,
        out_specs=(P(None, "row", None, None), P(None, "row", None, None)),
        check_vma=False,
    )
```

profile of v0, /device:TPU:1, one launch (start us, length us, event | category | flops | bytes accessed | tf_op | source)
XLA Modules:
  0.0 2463.4 jit_solution(8085514892885010404)
XLA Ops:
  7.2 1.4 fusion.117
  9.3 2.2 fusion.54
  11.6 0.7 fusion.106
  12.3 1.4 fusion.118
  13.6 1.3 compare_and_fusion
  14.9 25.7 %all-gather.7.cloned.1.call-done = bf16[2048,512]{1,0:T(8,128)(2,1)} async-done(((bf16[256,512]{1,0:T(8,128)(2,1)}), bf16[2048,512]{1,0:T(8,128)(2,1)}) %all-gather.7.cloned.1.call-update) | async-done | bytes 2097168 | tf_op jit(solution)/shard_map/all_gather | solution.py:55
  40.7 4.1 gather_fusion
  44.7 6.5 fusion.39
  51.9 83.2 %all-reduce.4.cloned.1.call-done = f32[256,512]{1,0:T(8,128)} async-done(((f32[256,512]{1,0:T(8,128)}), f32[256,512]{1,0:T(8,128)}) %all-reduce.4.cloned.1.call-update) | async-done | bytes 524304 | tf_op jit(solution)/shard_map/psum | solution.py:49
  135.1 2.2 fusion.55
  138.0 26.0 %all-gather.9.cloned.1.call-done = bf16[2048,512]{1,0:T(8,128)(2,1)} async-done(((bf16[256,512]{1,0:T(8,128)(2,1)}), bf16[2048,512]{1,0:T(8,128)(2,1)}) %all-gather.9.cloned.1.call-update) | async-done | bytes 2097168 | tf_op jit(solution)/shard_map/all_gather | solution.py:55
  164.0 3.9 pad_maximum_fusion.1
  167.9 4.7 gather_fusion.1
  172.6 6.4 fusion.44
  179.7 83.2 %all-reduce.6.cloned.1.call-done = f32[256,512]{1,0:T(8,128)} async-done(((f32[256,512]{1,0:T(8,128)}), f32[256,512]{1,0:T(8,128)}) %all-reduce.6.cloned.1.call-update) | async-done | bytes 524304 | tf_op jit(solution)/shard_map/psum | solution.py:49
  262.8 2.3 fusion.56
  265.8 26.0 %all-gather.11.cloned.1.call-done = bf16[2048,512]{1,0:T(8,128)(2,1)} async-done(((bf16[256,512]{1,0:T(8,128)(2,1)}), bf16[2048,512]{1,0:T(8,128)(2,1)}) %all-gather.11.cloned.1.call-update) | async-done | bytes 2097168 | tf_op jit(solution)/shard_map/all_gather | solution.py:55
  291.8 5.5 pad_maximum_fusion
  297.3 5.3 gather_fusion.2
  302.6 6.5 fusion.49
  310.4 82.5 %all-reduce.8.cloned.1.call-done = f32[256,512]{1,0:T(8,128)} async-done(((f32[256,512]{1,0:T(8,128)}), f32[256,512]{1,0:T(8,128)}) %all-reduce.8.cloned.1.call-update) | async-done | bytes 524304 | tf_op jit(solution)/shard_map/psum | solution.py:49
  392.9 1.4 fusion.57
  394.3 0.7 copy-done.6
  395.3 7.3 multiply_bitcast_fusion.2
  402.7 7.9 broadcast_in_dim.46
  410.6 13.8 scatter_fusion
  424.3 2.9 slice.119
  427.3 2.7 copy.8
  430.6 628.9 %reduce-scatter.4.cloned.1.call-done = f32[16,512]{1,0:T(8,128)} async-done(((f32[2048,512]{1,0:T(8,128)}), f32[16,512]{1,0:T(8,128)}) %reduce-scatter.4.cloned.1.call-update) | async-done | bytes 32784 | tf_op jit(solution)/shard_map/reduce_scatter | solution.py:68
  1059.5 0.9 fusion.59
  1060.4 16.1 all_gather.21
  1076.5 7.2 multiply_bitcast_fusion.1
  1083.7 13.7 scatter_fusion.1
  1097.4 2.9 slice.120
  1100.3 2.7 copy.9
  1103.7 645.3 %reduce-scatter.6.cloned.1.call-done = f32[16,512]{1,0:T(8,128)} async-done(((f32[2048,512]{1,0:T(8,128)}), f32[16,512]{1,0:T(8,128)}) %reduce-scatter.6.cloned.1.call-update) | async-done | bytes 32784 | tf_op jit(solution)/shard_map/reduce_scatter | solution.py:68
  1749.0 0.9 fusion.60
  1750.0 15.8 all_gather.22
  1765.8 7.2 multiply_bitcast_fusion
  1773.0 13.5 scatter_fusion.2
  1786.5 2.9 slice.121
  1789.5 2.7 copy.10
  1792.2 0.9 copy-done.4
  1793.1 2.0 maximum_bitcast_fusion
  1795.1 642.9 %reduce-scatter.8.cloned.1.call-done = f32[16,512]{1,0:T(8,128)} async-done(((f32[2048,512]{1,0:T(8,128)}), f32[16,512]{1,0:T(8,128)}) %reduce-scatter.8.cloned.1.call-update) | async-done | bytes 32784 | tf_op jit(solution)/shard_map/reduce_scatter | solution.py:68
  2438.1 0.9 fusion.61
  2439.0 15.8 all_gather.23
  2454.8 2.1 maximum_bitcast_fusion.1
  (45 shorter events, 6.3 us)
Async XLA Ops:
  7.2 33.5 %all-gather.7.cloned.1.call-start = ((), (), s32[]{:S(2)}) async-start(), calls=%async_computation.9 | async-start | bytes 2359296 | tf_op jit(solution)/shard_map/all_gather | solution.py:55
  11.5 123.6 %all-reduce.4.cloned.1.call-start = ((), (), s32[]{:S(2)}) async-start(), calls=%async_computation.3 | async-start | bytes 1048576 | tf_op jit(solution)/shard_map/psum | solution.py:49
  44.7 90.3 %copy-start.7 = (bf16[4,1,256,512]{3,2,1,0:T(8,128)(2,1)S(1)}, bf16[4,1,256,512]{3,2,1,0:T(8,128)(2,1)}, u32[]{:S(2)}) copy-start(bf16[4,1,256,512]{3,2,1,0:T(8,128)(2,1)} %param.6) | copy-start | bytes 3145732
  44.7 119.3 %copy-start = (bf16[2048,512]{1,0:T(8,128)(2,1)S(1)}, bf16[2048,512]{1,0:T(8,128)(2,1)}, u32[]{:S(2)}) copy-start(bf16[2048,512]{1,0:T(8,128)(2,1)} %all-gather.7.cloned.1.call-done) | copy-start | bytes 6291460
  51.3 112.7 %all-gather.9.cloned.1.call-start = ((), (), s32[]{:S(2)}) async-start(), calls=%async_computation.10 | async-start | bytes 2359296 | tf_op jit(solution)/shard_map/all_gather | solution.py:55
  137.3 125.5 %all-reduce.6.cloned.1.call-start = ((), (), s32[]{:S(2)}) async-start(), calls=%async_computation.4 | async-start | bytes 1048576 | tf_op jit(solution)/shard_map/psum | solution.py:49
  179.0 112.8 %all-gather.11.cloned.1.call-start = ((), (), s32[]{:S(2)}) async-start(), calls=%async_computation.11 | async-start | bytes 2359296 | tf_op jit(solution)/shard_map/all_gather | solution.py:55
  265.1 127.8 %all-reduce.8.cloned.1.call-start = ((), (), s32[]{:S(2)}) async-start(), calls=%async_computation.5 | async-start | bytes 1048576 | tf_op jit(solution)/shard_map/psum | solution.py:49
  302.6 90.3 %copy-start.1 = (bf16[4,1,512,512]{3,2,1,0:T(8,128)(2,1)S(1)}, bf16[4,1,512,512]{3,2,1,0:T(8,128)(2,1)}, u32[]{:S(2)}) copy-start(bf16[4,1,512,512]{3,2,1,0:T(8,128)(2,1)} %param.7) | copy-start | bytes 6291460
  309.1 750.3 %reduce-scatter.4.cloned.1.call-start = ((), (), s32[]{:S(2)}) async-start(), calls=%async_computation.6 | async-start | bytes 4227072 | tf_op jit(solution)/shard_map/reduce_scatter | solution.py:68
  394.3 0.7 copy-start.6
  395.3 7.4 copy-start.5
  429.9 629.5 %copy-start.3 = (bf16[256,512]{1,0:T(8,128)(2,1)S(1)}, bf16[256,512]{1,0:T(8,128)(2,1)}, u32[]{:S(2)}) copy-start(bf16[256,512]{1,0:T(8,128)(2,1)} %fusion.56) | copy-start | bytes 786436
  430.0 1319.1 %reduce-scatter.6.cloned.1.call-start = ((), (), s32[]{:S(2)}) async-start(), calls=%async_computation.7 | async-start | bytes 4227072 | tf_op jit(solution)/shard_map/reduce_scatter | solution.py:68
  1103.0 646.0 %copy-start.2 = (bf16[256,512]{1,0:T(8,128)(2,1)S(1)}, bf16[256,512]{1,0:T(8,128)(2,1)}, u32[]{:S(2)}) copy-start(bf16[256,512]{1,0:T(8,128)(2,1)} %fusion.55) | copy-start | bytes 786436
  1103.0 1335.0 %reduce-scatter.8.cloned.1.call-start = ((), (), s32[]{:S(2)}) async-start(), calls=%async_computation.8 | async-start | bytes 4227072 | tf_op jit(solution)/shard_map/reduce_scatter | solution.py:68
  1792.1 0.9 copy-start.4
Sparse Core Ops, SparseCore 0:
  11.6 28.9 all-gather.6
  51.4 83.6 all-reduce.3
  137.5 26.4 all-gather.8
  179.1 83.6 all-reduce.5
  265.2 26.4 all-gather.10
  309.3 83.6 all-reduce.7
  430.1 629.3 reduce-scatter.3
  1103.1 645.8 reduce-scatter.5
  1792.3 645.7 reduce-scatter.7
where the time goes:
time: 2490 us; the launch traced here: 2460 us
  waiting for transfers between devices  2240 us (90%)
  other arithmetic  61.9 us (2%)
  matrix products  52.4 us (2%)
  blocking collectives  47.7 us (2%)
  local copies, waits for them, and re-layouts  43.2 us (2%)
    reduce_scatter x3, waiting for transfers between devices, shards(): lax.psum_scatter(arranged, ('layer', 'row', 'col'), scatter_dimension=0,...  1920 us
    psum x3, waiting for transfers between devices, shards(): total = lax.psum(partial_value, ('layer', 'col'))  249 us
    all_gather x3, waiting for transfers between devices, shards(): stash.append(lax.all_gather(solved[None], 'row', axis=0, tiled=True))  77.7 us
  transfers between devices with their start and end apart: 9, of which 9 were waited for; matrix products, arithmetic and copies ran while one was open for 0% of the time, Pallas kernels for 0%

commit v1 on v0

v1 whole, which is shorter than its diff:
```python
import jax
import jax.numpy as jnp
from jax import lax
from jax.experimental import pallas as pl
from jax.experimental.pallas import tpu as pltpu
from jax.sharding import PartitionSpec as P

MESH = pl.DeviceIdType.MESH
BF = jnp.bfloat16
F32 = jnp.float32
LEV = 4
SPD = 12
W = 512
H = 256
LINE = [(i, k, n) for n in range(2) for k in range(4) for i in range(4) if i or k or n]
NEAR = (1, 3, 2)


def rem4(v):
    return lax.rem(v, 4)


def kernel(
    rhs_ref, dinv_ref, factor_ref, deps_ref, counts_ref, sizes_ref,
    forward_ref, solution_ref,
    rhs_v, dinv_v, fac,
    ko0, ko1, ko2, kx0, kx1, kx2,
    share, fshare, part, acc, f1r,
    a_own, a_oth, sb, sr, os, r1, s2, rr, sol, fw3,
    prev, last,
    in_sem, fac_sem, out_sem,
    plane_send, f1_recv, ag_recv,
    line_send, s1_recv, rs2_recv,
    axis_send, f5_recv, rs1_recv,
    sib_send, f6_recv, sib_recv,
):
    layer, row, col = lax.axis_index("layer"), lax.axis_index("row"), lax.axis_index("col")
    x = rem4(col)
    y = layer * 2 + lax.div(col, 4)
    z = lax.div(row, 2)
    core = lax.rem(row, 2)
    other = 1 - core
    me = core * 4 + z
    know_own, know_oth = (ko0, ko1, ko2), (kx0, kx1, kx2)

    def device(i, j, k, n):
        xx, yy, zz, cc = rem4(x + i), rem4(y + j), rem4(z + k), lax.rem(core + n, 2)
        return (lax.div(yy, 2), zz * 2 + cc, lax.rem(yy, 2) * 4 + xx)

    def send(src, dst, send_sem, recv_sem, to):
        return pltpu.make_async_remote_copy(
            src_ref=src, dst_ref=dst, send_sem=send_sem, recv_sem=recv_sem,
            device_id=to, device_id_type=MESH,
        )

    loads = []
    for level in range(LEV):
        loads.append(pltpu.make_async_copy(
            rhs_ref.at[level, 0, pl.ds(pl.multiple_of((y * 4 + x) * 16, 16), 16)],
            rhs_v.at[level], in_sem.at[level, 0]))
        loads.append(pltpu.make_async_copy(dinv_ref.at[level, 0], dinv_v.at[level], in_sem.at[level, 1]))
    for copy in loads:
        copy.start()
    fac_loads = [
        pltpu.make_async_copy(factor_ref.at[m, 0, k], fac.at[m, k], fac_sem.at[m, k])
        for m in range(LEV - 1) for k in range(SPD)
    ]
    for copy in fac_loads:
        copy.start()

    barrier = pltpu.get_barrier_semaphore()
    partners = [
        (i, j, k, n) for i in range(4) for j in range(4) for k in range(4) for n in range(2)
        if (i or j or k or n) and (i == 0 or j == 0 or (k == 0 and n == 0))
    ]
    for p in partners:
        pl.semaphore_signal(barrier, inc=1, device_id=device(*p), device_id_type=MESH)

    def live_rows(level):
        return (lax.broadcasted_iota(jnp.int32, (1, W), 1) < sizes_ref[level, 0]).astype(F32)

    def plane(src, dst, recv_sem, own):
        copies = []
        for i in range(4):
            for j in range(4):
                if i or j:
                    copies.append(send(
                        src(rem4(y + j), rem4(x + i)), dst, plane_send.at[i, j],
                        recv_sem.at[i, j], device(i, j, 0, 0)))
        for copy in copies:
            copy.start()
        return copies

    def wait(copies):
        for copy in copies:
            copy.wait()

    def prepare():
        def one(m, carry):
            count = counts_ref[m, 0, 0]
            keys = [jnp.where(k < count, deps_ref[m, 0, k], 255) for k in range(SPD)]
            for k in range(SPD):
                at = jnp.int32(SPD)
                for j in range(k):
                    at = jnp.where(keys[j] == keys[k], j, at)
                prev[m, k] = at

            def target(t, carry):
                unit = lax.rem(t, 8)
                name = lax.div(t, 8) * 8 + rem4(unit) * 2 + lax.div(unit, 4)
                at = jnp.int32(SPD)
                for k in range(SPD):
                    at = jnp.where(keys[k] == name, k, at)
                last[m, t] = at
                return carry

            lax.fori_loop(0, 24, target, 0)
            return carry

        lax.fori_loop(0, LEV - 1, one, 0)
        for m in range(LEV - 1):
            a_own[m, SPD] = jnp.zeros((H, H), F32)
            a_oth[m, SPD] = jnp.zeros((H, H), F32)

    def solve_forward(level, resid):
        product = lax.dot_general(
            resid, dinv_v[level], (((1,), (1,)), ((), ())), preferred_element_type=F32)
        solved = (product * live_rows(level)).astype(BF)
        fshare[level] = solved
        return solved

    def gather_level(level, solved):
        own, oth = know_own[level], know_oth[level]
        share[level, 0] = solved[:, :H]
        share[level, 1] = solved[:, H:]
        own[me, y, x] = share[level, core]
        copies = []
        for i, k, n in LINE:
            half = lax.rem(core + n, 2)
            copies.append(send(
                share.at[level, half], own.at[me, y, x], line_send.at[n, k, i],
                s1_recv.at[level, core, k, i],
                device(i * core, i * (1 - core), k, n)))
        for copy in copies:
            copy.start()
        if level == 0:
            prepare()
        for copy in copies:
            copy.wait_send()
        for i, k, n in LINE:
            half = lax.rem(core + n, 2)
            send(share.at[level, half], own.at[me, y, x], line_send.at[n, k, i],
                 s1_recv.at[level, half, k, i], device(0, 0, 0, 1)).wait_recv()
        evens = lambda at: own.at[pl.ds(0, 4), :, at]
        odds = lambda at: own.at[pl.ds(4, 4), at]
        evens_oth = lambda at: oth.at[pl.ds(0, 4), :, at]
        odds_oth = lambda at: oth.at[pl.ds(4, 4), at]
        axis = []
        for i in NEAR:
            axis.append(send(evens(x), evens(x), axis_send.at[0, i], f5_recv.at[level, 0, i], device(i, 0, 0, 0)))
            axis.append(send(odds(y), odds(y), axis_send.at[1, i], f5_recv.at[level, 1, i], device(0, i, 0, 0)))
        for copy in axis:
            copy.start()
        sibling = []

        def pass_on(src, dst, p, i):
            copy = send(src, dst, sib_send.at[p, i], f6_recv.at[level, p, i], device(0, 0, 0, 1))
            copy.start()
            sibling.append(copy)

        pass_on(evens(x), evens_oth(x), 0, 0)
        pass_on(odds(y), odds_oth(y), 1, 0)
        for at, i in enumerate(NEAR):
            axis[2 * at].wait_recv()
            pass_on(evens(rem4(x + 4 - i)), evens_oth(rem4(x + 4 - i)), 0, i)
            axis[2 * at + 1].wait_recv()
            pass_on(odds(rem4(y + 4 - i)), odds_oth(rem4(y + 4 - i)), 1, i)
        for copy in axis:
            copy.wait_send()
        return sibling

    def accumulate(m, know, half):
        def slot(k, carry):
            dep = deps_ref[m - 1, 0, k]
            source = lax.div(dep, 8)
            r = lax.rem(dep, 8)
            unit = lax.rem(r, 2) * 4 + lax.div(r, 2)
            value = know[0][unit].reshape(H, H)
            for at in range(1, m):
                value = jnp.where(source == at, know[at][unit].reshape(H, H), value)
            value = jnp.where(k < counts_ref[m - 1, 0, 0], value, jnp.zeros_like(value))
            block = fac[m - 1, k, :, pl.ds(pl.multiple_of(half * H, H), H)]
            acc[...] += lax.dot_general(
                value, block, (((1,), (1,)), ((), ())), preferred_element_type=F32)
            return carry

        lax.fori_loop(0, SPD, slot, 0)

    for copy in loads[0:2]:
        copy.wait()
    solved = solve_forward(0, rhs_v[0])
    pl.semaphore_wait(barrier, len(partners))
    out_copies = []
    for level in range(LEV - 1):
        sibling = gather_level(level, solved)
        m = level + 1
        for copy in fac_loads[level * SPD : m * SPD]:
            copy.wait()
        acc[...] = jnp.zeros_like(acc)
        accumulate(m, know_own, core)
        wait(sibling)
        accumulate(m, know_oth, other)
        part[...] = acc[...].astype(BF).reshape(4, 4, 16, W)
        f1r[level, y, x] = part[y, x]
        copies = plane(lambda gy, gx: part.at[gy, gx], f1r.at[level, y, x], f1_recv.at[level], None)
        for half, know in ((core, know_own[level]), (other, know_oth[level])):
            out_copies.append(pltpu.make_async_copy(
                know.at[me],
                forward_ref.at[level, :, :, :, pl.ds(pl.multiple_of(half * H, H), H)],
                out_sem.at[len(out_copies)]))
            out_copies[-1].start()
        for copy in loads[2 * m : 2 * m + 2]:
            copy.wait()
        wait(copies)
        total = jnp.sum(f1r[level].astype(F32).reshape(16, 16, W), axis=0)
        solved = solve_forward(m, (rhs_v[m].astype(F32) - total).astype(BF))

    def solve_backward(level, resid):
        product = jnp.dot(resid, dinv_v[level], preferred_element_type=F32)
        return (product * live_rows(level)).astype(BF)

    def contributions(m, half, out):
        def slot(k, carry):
            block = fac[m - 1, k, :, pl.ds(pl.multiple_of(half * H, H), H)]
            term = jnp.dot(sol[m].reshape(H, W), block, preferred_element_type=F32)
            out[m - 1, k] = term + out[m - 1, prev[m - 1, k]]
            return carry

        lax.fori_loop(0, SPD, slot, 0)

    def gathered(level, unit, out):
        value = out[level, last[level, level * 8 + unit]]
        for m in range(level + 2, LEV):
            value = value + out[m - 1, last[m - 1, level * 8 + unit]]
        return value

    last_level = LEV - 1
    fw3[y, x] = solved
    solved = solve_backward(last_level, solved)
    for level in range(last_level, -1, -1):
        sol[level, y, x] = solved
        copies = plane(lambda gy, gx: sol.at[level, y, x], sol.at[level, y, x], ag_recv.at[level], None)
        wait(copies)
        if level == last_level:
            fw_copies = plane(lambda gy, gx: fw3.at[y, x], fw3.at[y, x], f1_recv.at[last_level], None)
        out_copies.append(pltpu.make_async_copy(
            sol.at[level], solution_ref.at[level], out_sem.at[len(out_copies)]))
        out_copies[-1].start()
        if level == 0:
            break
        low = level - 1
        contributions(level, other, a_oth)
        sibling = []

        def to_sibling(unit, carry):
            sb[unit] = gathered(low, unit, a_oth).astype(BF).reshape(4, 4, 16, H)
            send(sb.at[unit], sr.at[unit], sib_send.at[lax.div(unit, 4), rem4(unit)],
                 sib_recv.at[low, unit], device(0, 0, 0, 1)).start()
            return carry

        lax.fori_loop(0, 8, to_sibling, 0)
        contributions(level, core, a_own)

        def from_sibling(unit, carry):
            send(sb.at[unit], sr.at[unit], sib_send.at[lax.div(unit, 4), rem4(unit)],
                 sib_recv.at[low, unit], device(0, 0, 0, 1)).wait()
            both = gathered(low, unit, a_own) + sr[unit].reshape(H, H).astype(F32)
            os[unit] = both.astype(BF).reshape(4, 4, 16, H)
            return carry

        lax.fori_loop(0, 4, from_sibling, 0)
        axis = []
        for i in NEAR:
            axis.append(send(os.at[pl.ds(0, 4), :, rem4(x + i)], r1.at[0, i - 1],
                             axis_send.at[0, i], rs1_recv.at[low, 0, i], device(i, 0, 0, 0)))
        for copy in axis:
            copy.start()
        lax.fori_loop(4, 8, from_sibling, 0)
        for i in NEAR:
            axis.append(send(os.at[pl.ds(4, 4), rem4(y + i)], r1.at[1, i - 1],
                             axis_send.at[1, i], rs1_recv.at[low, 1, i], device(0, i, 0, 0)))
        for copy in axis[3:]:
            copy.start()
        if level == last_level:
            wait(fw_copies)
            out_copies.append(pltpu.make_async_copy(
                fw3, forward_ref.at[last_level], out_sem.at[len(out_copies)]))
            out_copies[-1].start()
        wait(axis[:3])
        for k in range(4):
            s2[0, k] = (os[k, :, x].astype(F32) + r1[0, 0, k].astype(F32)
                        + r1[0, 1, k].astype(F32) + r1[0, 2, k].astype(F32)).astype(BF)
        wait(axis[3:])
        for k in range(4):
            s2[1, k] = (os[4 + k, y].astype(F32) + r1[1, 0, k].astype(F32)
                        + r1[1, 1, k].astype(F32) + r1[1, 2, k].astype(F32)).astype(BF)
        copies = []
        for i, k, n in LINE:
            to = lax.rem(core + n, 2)
            at = rem4(x * to + y * (1 - to) + i)
            copies.append(send(
                s2.at[to, rem4(z + k), at], rr.at[low, core, k, i], line_send.at[n, k, i],
                rs2_recv.at[low, core, k, i], device(i * to, i * (1 - to), k, n)))
        for copy in copies:
            copy.start()
        rr[low, core, 0, 0] = s2[core, z, rem4(x * core + y * (1 - core))]
        for copy in copies:
            copy.wait_send()
        for i, k, n in LINE:
            half = lax.rem(core + n, 2)
            send(s2.at[0, 0, 0], rr.at[low, half, k, i], line_send.at[n, k, i],
                 rs2_recv.at[low, half, k, i], device(0, 0, 0, 1)).wait_recv()
        sums = [jnp.sum(rr[low, half].astype(F32).reshape(16, 16, H), axis=0) for half in range(2)]
        total = jnp.concatenate(sums, axis=1)
        solved = solve_backward(low, (fshare[low].astype(F32) - total).astype(BF))
    for copy in out_copies:
        copy.wait()


def shards(rhs, dinv, factor, deps, counts, sizes):
    any_spec = pl.BlockSpec(memory_space=pl.ANY)
    smem = pl.BlockSpec(memory_space=pltpu.SMEM)
    dma = pltpu.SemaphoreType.DMA
    block = (8, 4, 4, 16, H)
    forward, solved = pl.pallas_call(
        kernel,
        out_shape=[jax.ShapeDtypeStruct((LEV, 4, 4, 16, W), BF)] * 2,
        in_specs=[any_spec] * 3 + [smem] * 3,
        out_specs=[any_spec] * 2,
        scratch_shapes=[
            pltpu.VMEM((LEV, 16, W), BF),
            pltpu.VMEM((LEV, W, W), BF),
            pltpu.VMEM((LEV - 1, SPD, W, W), BF),
        ] + [pltpu.VMEM(block, BF)] * 6 + [
            pltpu.VMEM((LEV, 2, 16, H), BF),
            pltpu.VMEM((LEV, 16, W), BF),
            pltpu.VMEM((4, 4, 16, W), BF),
            pltpu.VMEM((H, W), F32),
            pltpu.VMEM((LEV - 1, 4, 4, 16, W), BF),
            pltpu.VMEM((LEV - 1, SPD + 1, H, H), F32),
            pltpu.VMEM((LEV - 1, SPD + 1, H, H), F32),
            pltpu.VMEM(block, BF),
            pltpu.VMEM(block, BF),
            pltpu.VMEM(block, BF),
            pltpu.VMEM((2, 3, 4, 4, 16, H), BF),
            pltpu.VMEM((2, 4, 4, 16, H), BF),
            pltpu.VMEM((LEV - 1, 2, 4, 4, 16, H), BF),
            pltpu.VMEM((LEV, 4, 4, 16, W), BF),
            pltpu.VMEM((4, 4, 16, W), BF),
            pltpu.SMEM((LEV - 1, SPD), jnp.int32),
            pltpu.SMEM((LEV - 1, 24), jnp.int32),
            dma((LEV, 2)), dma((LEV - 1, SPD)), dma((12,)),
            dma((4, 4)), dma((LEV, 4, 4)), dma((LEV, 4, 4)),
            dma((2, 4, 4)), dma((LEV - 1, 2, 4, 4)), dma((LEV - 1, 2, 4, 4)),
            dma((2, 4)), dma((LEV - 1, 2, 4)), dma((LEV - 1, 2, 4)),
            dma((2, 4)), dma((LEV - 1, 2, 4)), dma((LEV - 1, 8)),
        ],
        compiler_params=pltpu.CompilerParams(
            collective_id=0, has_side_effects=True, vmem_limit_bytes=60 << 20),
        name="levels",
    )(rhs, dinv, factor, deps, counts, sizes)
    return forward.reshape(LEV, 1, H, W), solved.reshape(LEV, 1, H, W)


def solution(mesh):
    placed = (
        P(None, "row", None, None),
        P(None, "row", None, None),
        P(None, "row", ("layer", "col"), None, None),
        P(None, "row", ("layer", "col")),
        P(None, "row", ("layer", "col")),
        P(None, "row"),
    )
    return jax.shard_map(
        shards,
        mesh=mesh,
        in_specs=placed,
        out_specs=(P(None, "row", None, None), P(None, "row", None, None)),
        check_vma=False,
    )
```

time: 2490 us -> 189 us (0.08); the launches traced: 2460 us -> 189 us
  waiting for transfers between devices: 2240 us -> 0 us
  Pallas kernels: 0 us -> 181 us
  other arithmetic: 61.9 us -> 0 us
  matrix products: 52.4 us -> 0 us
  blocking collectives: 47.7 us -> 0 us
  local copies, waits for them, and re-layouts: 43.2 us -> 7.13 us
    reduce_scatter x3 -> x0, waiting for transfers between devices: 1920 us -> none  [shards(): lax.psum_scatter(arranged, ('layer', 'row', 'col'), scatter_dimension=0,...]
    psum x3 -> x0, waiting for transfers between devices: 249 us -> none  [shards(): total = lax.psum(partial_value, ('layer', 'col'))]
    pallas_call x0 -> x1, Pallas kernels: none -> 181 us  [shards(): pl.pallas_call(kernel, out_shape=[jax.ShapeDtypeStruct((LEV, 4, 4, 16, W)...]
    all_gather x3 -> x0, waiting for transfers between devices: 77.7 us -> none  [shards(): stash.append(lax.all_gather(solved[None], 'row', axis=0, tiled=True))]
    dot_general x14 -> x0, matrix products: 52.4 us -> none  [the longest x3 21.8 us: shards(): jnp.einsum('nj,kji->kni', solved, factor[level - 1, 0], preferred_element...]
    all_gather x3 -> x0, blocking collectives: 47.7 us -> none  [shards(): solved = lax.all_gather(piece, ('layer', 'col'), axis=0, tiled=True)]
    scatter-add x3 -> x0, other arithmetic: 41 us -> none  [shards(): carried = carried.at[deps[level - 1, 0]].add(terms)]
  transfers between devices with their start and end apart: 9 -> 0, of which waited for: 9 -> 0; matrix products, arithmetic and copies ran while one was open for 0% -> 0% of each run, Pallas kernels for 0% -> 0%
where the time goes in v1:
time: 189 us
  Pallas kernels  181 us (96%)
  local copies, waits for them, and re-layouts  7.13 us (4%)
    pallas_call x1, Pallas kernels, shards(): pl.pallas_call(kernel, out_shape=[jax.ShapeDtypeStruct((LEV, 4, 4, 16, W)...  181 us
    unnamed x4, local copies, waits for them, and re-layouts  7.13 us

profile of v1, /device:TPU:1, one launch (start us, length us, event | category | flops | bytes accessed | tf_op | source)
XLA Modules:
  0.0 189.1 jit_solution(14407370669547558411)
XLA Ops:
  0.6 1.3 copy.8.counts_ref
  1.9 1.3 copy.9.sizes_ref
  3.2 181.3 %levels.1 = (bf16[4,4,4,16,512]{4,3,2,1,0:T(8,128)(2,1)}, bf16[4,4,4,16,512]{4,3,2,1,0:T(8,128)(2,1)}) custom-call(bf16[4,1,256,512]{3,2,1,0:T(8,128)(2,1)} %rhs_ref.1, bf16[4,1,512,512]{3,2,1,0:T(8,128)(2,1)} %dinv_ref.1, bf16[3,1,12,512,512]{4,3,2,1,0:T(8,128)(2,1)} %factor_ref.1, s32[3,1,12]{2,1,0:T(1,128)} %deps_ref.1, s32[3,1,1]{2,1,0:T(1,128)} %copy.8.counts_ref, ...), custom_call_target="tpu_custom_call" | custom-call | tf_op jit(solution)/shard_map/levels/pallas_call | solution.py:335
  184.6 2.3 %copy.14 = bf16[4,1,256,512]{3,2,1,0:T(8,128)(2,1)} copy(bf16[4,1,256,512]{3,2,1,0:T(8,128)(2,1)} %bitcast.7) | data formatting | bytes 2097152
  186.8 2.3 %copy.15 = bf16[4,1,256,512]{3,2,1,0:T(8,128)(2,1)} copy(bf16[4,1,256,512]{3,2,1,0:T(8,128)(2,1)} %bitcast.6) | data formatting | bytes 2097152

commit v2 on v0

v2 whole, which is shorter than its diff:
```python
import jax
import jax.numpy as jnp
from jax import lax
from jax.experimental import pallas as pl
from jax.experimental.pallas import tpu as pltpu
from jax.sharding import PartitionSpec as P

MESH = pl.DeviceIdType.MESH
BF = jnp.bfloat16
F32 = jnp.float32
LEV = 4
SPD = 12
W = 512
H = 256
UNROLL = 4


def rem4(v):
    return lax.rem(v, 4)


def near_first(v):
    return v + lax.div(v, 2) * (5 - 2 * v)


def kernel(
    rhs_ref, dinv_ref, factor_ref, deps_ref, counts_ref, sizes_ref,
    forward_ref, solution_ref,
    rhs_v, dinv_v, fac, ko, kx, kl,
    share, fshare, part, acc, f1r,
    a, sb, sr, os, r1, s2, rr, sol, fw3,
    prev, last,
    rhs_sem, dinv_sem, fac_sem, fout_sem, sout_sem,
    plane_send, fw3_send, f1_recv, ag_recv, fw3_recv,
    line_send, s1_recv, rs2_recv,
    axis_send, f5_recv, rs1_recv,
    sib_send, f6_recv, sib_recv,
):
    layer, row, col = lax.axis_index("layer"), lax.axis_index("row"), lax.axis_index("col")
    x = rem4(col)
    y = layer * 2 + lax.div(col, 4)
    z = lax.div(row, 2)
    core = lax.rem(row, 2)
    other = 1 - core
    me = core * 4 + z
    line = x * core + y * other

    def device(i, j, k, n):
        xx, yy, zz, cc = rem4(x + i), rem4(y + j), rem4(z + k), lax.rem(core + n, 2)
        return (lax.div(yy, 2), zz * 2 + cc, lax.rem(yy, 2) * 4 + xx)

    def send(src, dst, send_sem, recv_sem, to):
        return pltpu.make_async_remote_copy(
            src_ref=src, dst_ref=dst, send_sem=send_sem, recv_sem=recv_sem,
            device_id=to, device_id_type=MESH,
        )

    def each(low, high, body):
        def step(at, carry):
            body(at)
            return carry
        lax.fori_loop(low, high, step, 0)

    def rows(gy, gx):
        return pl.ds(pl.multiple_of((gy * 4 + gx) * 16, 16), 16)

    def half_cols(half):
        return pl.ds(pl.multiple_of(half * H, H), H)

    mine = rows(y, x)

    def rhs_load(level):
        return pltpu.make_async_copy(rhs_ref.at[level, 0, mine], rhs_v.at[level], rhs_sem.at[level])

    def dinv_load(level):
        return pltpu.make_async_copy(dinv_ref.at[level, 0], dinv_v.at[level], dinv_sem.at[level])

    def fac_load(m):
        return pltpu.make_async_copy(factor_ref.at[m, 0], fac.at[m], fac_sem.at[m])

    def start_loads(level):
        rhs_load(level).start()
        dinv_load(level).start()

    each(0, LEV, start_loads)
    each(0, LEV - 1, lambda m: fac_load(m).start())

    barrier = pltpu.get_barrier_semaphore()

    def greet(i, j, k, n):
        pl.semaphore_signal(barrier, inc=1, device_id=device(i, j, k, n), device_id_type=MESH)

    each(1, 16, lambda o: greet(rem4(o), lax.div(o, 4), 0, 0))
    each(4, 32, lambda o: greet(0, rem4(o), lax.div(o, 8), lax.rem(lax.div(o, 4), 2)))
    each(3, 24, lambda o: greet(
        1 + lax.rem(o, 3), 0, lax.div(o, 6), lax.rem(lax.div(o, 3), 2)))

    def live_rows(level):
        return (lax.broadcasted_iota(jnp.int32, (1, W), 1) < sizes_ref[0, level]).astype(F32)

    def plane_copy(o, src, dst, send_sem, recv_sem):
        i, j = rem4(o), lax.div(o, 4)
        return send(src(rem4(y + j), rem4(x + i)), dst, send_sem.at[o], recv_sem.at[o], device(i, j, 0, 0))

    def part_copy(level):
        return lambda o: plane_copy(
            o, lambda gy, gx: part.at[rows(gy, gx)], f1r.at[level, mine], plane_send, f1_recv.at[level])

    def sol_copy(level):
        return lambda o: plane_copy(
            o, lambda gy, gx: sol.at[level, mine], sol.at[level, mine], plane_send, ag_recv.at[level])

    def fw3_copy(o):
        return plane_copy(o, lambda gy, gx: fw3.at[mine], fw3.at[mine], fw3_send, fw3_recv)

    def prepare():
        def one(m):
            count = counts_ref[0, 0, m]
            keys = [jnp.where(k < count, deps_ref[m, 0, k], 255) for k in range(SPD)]
            for k in range(SPD):
                at = jnp.int32(SPD)
                for j in range(k):
                    at = jnp.where(keys[j] == keys[k], j, at)
                prev[m, k] = at

            def target(t):
                unit = lax.rem(t, 8)
                name = lax.div(t, 8) * 8 + rem4(unit) * 2 + lax.div(unit, 4)
                at = jnp.int32(SPD)
                for k in range(SPD):
                    at = jnp.where(keys[k] == name, k, at)
                last[m, t] = at

            each(0, 24, target)
            a[0, m, SPD] = jnp.zeros((H, H), F32)
            a[1, m, SPD] = jnp.zeros((H, H), F32)

        each(0, LEV - 1, one)

    def solve_forward(level, resid):
        product = lax.dot_general(
            resid, dinv_v[level], (((1,), (1,)), ((), ())), preferred_element_type=F32)
        solved = (product * live_rows(level)).astype(BF)
        fshare[level] = solved
        share[level, 0] = solved[:, :H]
        share[level, 1] = solved[:, H:]

    def accumulate(m, which, half):
        def slot(k, carry):
            dep = deps_ref[m - 1, 0, k]
            r = lax.rem(dep, 8)
            at = dep - r + lax.rem(r, 2) * 4 + lax.div(r, 2)
            value = kl[which, at]
            value = jnp.where(k < counts_ref[0, 0, m - 1], value, jnp.zeros_like(value))
            block = fac[m - 1, k, :, half_cols(half)]
            acc[...] += lax.dot_general(
                value, block, (((1,), (1,)), ((), ())), preferred_element_type=F32)
            return carry

        lax.fori_loop(0, SPD, slot, 0, unroll=UNROLL)

    def forward_out(level, which):
        half = core + which - 2 * core * which
        return pltpu.make_async_copy(
            kl.at[which, level * 8 + me], forward_ref.at[level, :, half_cols(half)],
            fout_sem.at[level, which])

    def forward_level(level):
        slot = lax.rem(level, 2)
        m = level + 1

        def s1(o):
            k, n, i = near_first(lax.div(o, 8)), lax.rem(lax.div(o, 4), 2), rem4(o)
            half = lax.rem(core + n, 2)
            return send(
                share.at[level, half], ko.at[slot, me, y, x], line_send.at[o],
                s1_recv.at[level, core, k, i], device(i * core, i * other, k, n))

        def s1_arrival(k, n, i):
            half = lax.rem(core + n, 2)
            return send(
                share.at[level, half], ko.at[slot, me, y, x], line_send.at[0],
                s1_recv.at[level, half, k, i], device(0, 0, 0, 1))

        def evens(ref, zc, at):
            return ref.at[slot, zc, :, at]

        def odds(ref, zc, at):
            return ref.at[slot, 4 + zc, at]

        def f5(p, k, i):
            zc = rem4(z + 4 - k)
            if p == 0:
                src, to = evens(ko, zc, x), device(i, 0, 0, 0)
            else:
                src, to = odds(ko, zc, y), device(0, i, 0, 0)
            return send(src, src, axis_send.at[p, k, i], f5_recv.at[level, p, k, i], to)

        def f6(p, k, i):
            zc = rem4(z + 4 - k)
            if p == 0:
                at = rem4(x + 4 - i)
                src, dst = evens(ko, zc, at), evens(kx, zc, at)
            else:
                at = rem4(y + 4 - i)
                src, dst = odds(ko, zc, at), odds(kx, zc, at)
            return send(src, dst, sib_send.at[p, k, i], f6_recv.at[level, p, k, i], device(0, 0, 0, 1))

        ko[slot, me, y, x] = share[level, core]
        each(1, 32, lambda o: s1(o).start())

        @pl.when(level == 0)
        def _():
            prepare()

        def chunk(kk):
            k = near_first(kk)
            first = jnp.where(kk == 0, 1, 0)
            each(first, 8, lambda q: s1_arrival(k, lax.div(q, 4), rem4(q)).wait_recv())

            def go(v):
                i = near_first(v)
                f5(0, k, i).start()
                f5(1, k, i).start()

            each(1, 4, go)
            f6(0, k, 0).start()
            f6(1, k, 0).start()

        each(0, 4, chunk)

        def relay(v):
            k, i = near_first(lax.div(v, 3)), near_first(1 + lax.rem(v, 3))
            for p in (0, 1):
                f5(p, k, i).wait_recv()
                f6(p, k, i).start()

        each(0, 12, relay)

        def keep_own(u):
            kl[0, level * 8 + u] = ko[slot, u].reshape(H, H)

        def keep_other(u):
            kl[1, level * 8 + u] = kx[slot, u].reshape(H, H)

        each(0, 8, keep_own)
        fac_load(level).wait()
        acc[...] = jnp.zeros_like(acc)

        def half_pass(which):
            @pl.when(which == 1)
            def _():
                def arrival(v):
                    for p in (0, 1):
                        f6(p, lax.div(v, 4), rem4(v)).wait_recv()
                each(0, 16, arrival)
                each(0, 8, keep_other)
            accumulate(m, which, lax.rem(core + which, 2))

        each(0, 2, half_pass)
        part[...] = acc[...].astype(BF)
        each(1, 16, lambda o: part_copy(level)(o).start())
        f1r[level, mine] = part[mine]
        for which in (0, 1):
            forward_out(level, which).start()
        each(1, 32, lambda o: s1(o).wait_send())

        def sent(v):
            for p in (0, 1):
                f5(p, lax.div(v, 3), 1 + lax.rem(v, 3)).wait_send()

        def passed(v):
            for p in (0, 1):
                f6(p, lax.div(v, 4), rem4(v)).wait_send()

        each(0, 12, sent)
        each(0, 16, passed)
        rhs_load(m).wait()
        dinv_load(m).wait()
        each(1, 16, lambda o: part_copy(level)(o).wait())
        total = jnp.sum(f1r[level].astype(F32).reshape(16, 16, W), axis=0)
        solve_forward(m, (rhs_v[m].astype(F32) - total).astype(BF))

    rhs_load(0).wait()
    dinv_load(0).wait()
    solve_forward(0, rhs_v[0])
    pl.semaphore_wait(barrier, 64)
    each(0, LEV - 1, forward_level)

    def solve_backward(level, resid):
        product = jnp.dot(resid, dinv_v[level], preferred_element_type=F32)
        sol[level, mine] = (product * live_rows(level)).astype(BF)

    def solution_out(level):
        return pltpu.make_async_copy(sol.at[level], solution_ref.at[level], sout_sem.at[level])

    def gather_plane(level):
        each(1, 16, lambda o: sol_copy(level)(o).start())
        each(1, 16, lambda o: sol_copy(level)(o).wait())
        solution_out(level).start()

    def backward_level(it):
        level = LEV - 1 - it
        low = level - 1
        gather_plane(level)

        @pl.when(it == 0)
        def _():
            each(1, 16, lambda o: fw3_copy(o).start())

        def gathered(unit, which):
            value = a[which, 0, last[0, low * 8 + unit]]
            for m in range(1, LEV - 1):
                value = value + a[which, m, last[m, low * 8 + unit]]
            return value

        def pair(unit):
            return send(sb.at[unit], sr.at[unit], sib_send.at[lax.div(unit, 4), rem4(unit), 0],
                        sib_recv.at[low, unit], device(0, 0, 0, 1))

        def far_first(kk):
            return near_first(3 - kk)

        def to_sibling(q):
            unit = lax.rem(q, 2) * 4 + rem4(z + far_first(lax.div(q, 2)))
            sb[unit] = gathered(unit, 0).astype(BF).reshape(4, 4, 16, H)
            pair(unit).start()

        def contributions(which):
            half = lax.rem(core + 1 + which, 2)

            def slot(k, carry):
                block = fac[low, k, :, half_cols(half)]
                term = jnp.dot(sol[level], block, preferred_element_type=F32)
                a[which, low, k] = term + a[which, low, prev[low, k]]
                return carry

            lax.fori_loop(0, SPD, slot, 0, unroll=UNROLL)

            @pl.when(which == 0)
            def _():
                each(0, 8, to_sibling)

        each(0, 2, contributions)

        def rs1(p, k, i):
            zc = rem4(z + k)
            if p == 0:
                src, to = os.at[zc, :, rem4(x + i)], device(i, 0, 0, 0)
            else:
                src, to = os.at[4 + zc, rem4(y + i)], device(0, i, 0, 0)
            return send(src, r1.at[p, i - 1, zc], axis_send.at[p, k, i], rs1_recv.at[low, p, k, i], to)

        def merge(kk):
            k = far_first(kk)
            zc = rem4(z + k)
            for p in (0, 1):
                unit = p * 4 + zc
                pair(unit).wait()
                both = gathered(unit, 1) + sr[unit].reshape(H, H).astype(F32)
                os[unit] = both.astype(BF).reshape(4, 4, 16, H)
                each(1, 4, lambda v: rs1(p, k, v).start())

        each(0, 4, merge)

        def rs2(o):
            k, n, i = lax.div(o, 8), lax.rem(lax.div(o, 4), 2), rem4(o)
            to = lax.rem(core + n, 2)
            at = rem4(x * to + y * (1 - to) + i)
            return send(
                s2.at[to, rem4(z + k), at], rr.at[low, core, k, i], line_send.at[o],
                rs2_recv.at[low, core, k, i], device(i * to, i * (1 - to), k, n))

        def rs2_arrival(o):
            k, n, i = lax.div(o, 8), lax.rem(lax.div(o, 4), 2), rem4(o)
            half = lax.rem(core + n, 2)
            return send(
                s2.at[0, 0, 0], rr.at[low, half, k, i], line_send.at[0],
                rs2_recv.at[low, half, k, i], device(0, 0, 0, 1))

        def fold(kk):
            k = far_first(kk)
            zc = rem4(z + k)
            for p in (0, 1):
                each(1, 4, lambda v: rs1(p, k, v).wait())
                value = os[zc, :, x] if p == 0 else os[4 + zc, y]
                value = value.astype(F32)
                for i in range(3):
                    value = value + r1[p, i, zc].astype(F32)
                s2[p, zc] = value.astype(BF)
            first = jnp.where(kk == 3, 1, 0)
            each(first, 8, lambda q: rs2(k * 8 + q).start())

        each(0, 4, fold)
        rr[low, core, 0, 0] = s2[core, z, line]
        each(1, 32, lambda o: rs2(o).wait_send())
        each(1, 32, lambda o: rs2_arrival(o).wait_recv())
        sums = [jnp.sum(rr[low, half].astype(F32).reshape(16, 16, H), axis=0) for half in range(2)]
        total = jnp.concatenate(sums, axis=1)
        solve_backward(low, (fshare[low].astype(F32) - total).astype(BF))

    fw3[mine] = fshare[LEV - 1]
    solve_backward(LEV - 1, fshare[LEV - 1])
    each(0, LEV - 1, backward_level)
    gather_plane(0)
    each(1, 16, lambda o: fw3_copy(o).wait())
    fw3_out = pltpu.make_async_copy(fw3, forward_ref.at[LEV - 1], fout_sem.at[LEV - 1, 0])
    fw3_out.start()
    each(0, LEV, lambda level: solution_out(level).wait())
    for which in (0, 1):
        each(0, LEV - 1, lambda level: forward_out(level, which).wait())
    fw3_out.wait()


def shards(rhs, dinv, factor, deps, counts, sizes):
    any_spec = pl.BlockSpec(memory_space=pl.ANY)
    smem = pl.BlockSpec(memory_space=pltpu.SMEM)
    dma = pltpu.SemaphoreType.DMA
    block = (8, 4, 4, 16, H)
    forward, solved = pl.pallas_call(
        kernel,
        out_shape=[jax.ShapeDtypeStruct((LEV, H, W), BF)] * 2,
        in_specs=[any_spec] * 3 + [smem] * 3,
        out_specs=[any_spec] * 2,
        scratch_shapes=[
            pltpu.VMEM((LEV, 16, W), BF),
            pltpu.VMEM((LEV, W, W), BF),
            pltpu.VMEM((LEV - 1, SPD, W, W), BF),
            pltpu.VMEM((2,) + block, BF),
            pltpu.VMEM((2,) + block, BF),
            pltpu.VMEM((2, 24, H, H), BF),
            pltpu.VMEM((LEV, 2, 16, H), BF),
            pltpu.VMEM((LEV, 16, W), BF),
            pltpu.VMEM((H, W), BF),
            pltpu.VMEM((H, W), F32),
            pltpu.VMEM((LEV - 1, H, W), BF),
            pltpu.VMEM((2, LEV - 1, SPD + 1, H, H), F32),
            pltpu.VMEM(block, BF),
            pltpu.VMEM(block, BF),
            pltpu.VMEM(block, BF),
            pltpu.VMEM((2, 3, 4, 4, 16, H), BF),
            pltpu.VMEM((2, 4, 4, 16, H), BF),
            pltpu.VMEM((LEV - 1, 2, 4, 4, 16, H), BF),
            pltpu.VMEM((LEV, H, W), BF),
            pltpu.VMEM((H, W), BF),
            pltpu.SMEM((LEV - 1, SPD), jnp.int32),
            pltpu.SMEM((LEV - 1, 24), jnp.int32),
            dma((LEV,)), dma((LEV,)), dma((LEV - 1,)), dma((LEV, 2)), dma((LEV,)),
            dma((16,)), dma((16,)), dma((LEV - 1, 16)), dma((LEV, 16)), dma((16,)),
            dma((32,)), dma((LEV - 1, 2, 4, 4)), dma((LEV - 1, 2, 4, 4)),
            dma((2, 4, 4)), dma((LEV - 1, 2, 4, 4)), dma((LEV - 1, 2, 4, 4)),
            dma((2, 4, 4)), dma((LEV - 1, 2, 4, 4)), dma((LEV - 1, 8)),
        ],
        compiler_params=pltpu.CompilerParams(
            collective_id=0, has_side_effects=True, vmem_limit_bytes=61 << 20),
        name="levels",
    )(rhs, dinv, factor, deps, counts.transpose(1, 2, 0), sizes.T)
    return forward[:, None], solved[:, None]


def solution(mesh):
    placed = (
        P(None, "row", None, None),
        P(None, "row", None, None),
        P(None, "row", ("layer", "col"), None, None),
        P(None, "row", ("layer", "col")),
        P(None, "row", ("layer", "col")),
        P(None, "row"),
    )
    return jax.shard_map(
        shards,
        mesh=mesh,
        in_specs=placed,
        out_specs=(P(None, "row", None, None), P(None, "row", None, None)),
        check_vma=False,
    )
```

time: 2490 us -> 161 us (0.06); the launches traced: 2460 us -> 161 us
  waiting for transfers between devices: 2240 us -> 0 us
  Pallas kernels: 0 us -> 156 us
  other arithmetic: 61.9 us -> 0 us
  matrix products: 52.4 us -> 0 us
  blocking collectives: 47.7 us -> 0 us
  local copies, waits for them, and re-layouts: 43.2 us -> 4.52 us
    reduce_scatter x3 -> x0, waiting for transfers between devices: 1920 us -> none  [shards(): lax.psum_scatter(arranged, ('layer', 'row', 'col'), scatter_dimension=0,...]
    psum x3 -> x0, waiting for transfers between devices: 249 us -> none  [shards(): total = lax.psum(partial_value, ('layer', 'col'))]
    pallas_call x0 -> x1, Pallas kernels: none -> 156 us  [shards(): pl.pallas_call(kernel, out_shape=[jax.ShapeDtypeStruct((LEV, H, W), BF)]...]
    all_gather x3 -> x0, waiting for transfers between devices: 77.7 us -> none  [shards(): stash.append(lax.all_gather(solved[None], 'row', axis=0, tiled=True))]
    dot_general x14 -> x0, matrix products: 52.4 us -> none  [the longest x3 21.8 us: shards(): jnp.einsum('nj,kji->kni', solved, factor[level - 1, 0], preferred_element...]
    all_gather x3 -> x0, blocking collectives: 47.7 us -> none  [shards(): solved = lax.all_gather(piece, ('layer', 'col'), axis=0, tiled=True)]
    scatter-add x3 -> x0, other arithmetic: 41 us -> none  [shards(): carried = carried.at[deps[level - 1, 0]].add(terms)]
  transfers between devices with their start and end apart: 9 -> 0, of which waited for: 9 -> 0; matrix products, arithmetic and copies ran while one was open for 0% -> 0% of each run, Pallas kernels for 0% -> 0%
where the time goes in v2:
time: 161 us
  Pallas kernels  156 us (97%)
  local copies, waits for them, and re-layouts  4.52 us (3%)
    pallas_call x1, Pallas kernels, shards(): pl.pallas_call(kernel, out_shape=[jax.ShapeDtypeStruct((LEV, H, W), BF)]...  156 us
    unnamed x2, local copies, waits for them, and re-layouts  4.52 us

profile of v2, /device:TPU:1, one launch (start us, length us, event | category | flops | bytes accessed | tf_op | source)
XLA Modules:
  0.0 160.8 jit_solution(11574217496032884208)
XLA Ops:
  0.6 155.6 %levels.1 = (bf16[4,256,512]{2,1,0:T(8,128)(2,1)}, bf16[4,256,512]{2,1,0:T(8,128)(2,1)}) custom-call(bf16[4,1,256,512]{3,2,1,0:T(8,128)(2,1)} %rhs_ref.1, bf16[4,1,512,512]{3,2,1,0:T(8,128)(2,1)} %dinv_ref.1, bf16[3,1,12,512,512]{4,3,2,1,0:T(8,128)(2,1)} %factor_ref.1, s32[3,1,12]{2,1,0:T(1,128)} %deps_ref.1, s32[1,1,3]{2,1,0:T(1,128)} %bitcast.10, ...), custom_call_target="tpu_custom_call" | custom-call | tf_op jit(solution)/shard_map/levels/pallas_call | solution.py:420
  156.3 2.3 %copy.12 = bf16[4,1,256,512]{3,2,1,0:T(8,128)(2,1)} copy(bf16[4,1,256,512]{3,2,1,0:T(8,128)(2,1)} %bitcast.9) | data formatting | bytes 2097152
  158.5 2.3 %copy.13 = bf16[4,1,256,512]{3,2,1,0:T(8,128)(2,1)} copy(bf16[4,1,256,512]{3,2,1,0:T(8,128)(2,1)} %bitcast.8) | data formatting | bytes 2097152

commit v3 on v2

--- a/solution.py
+++ b/solution.py
@@ -29,7 +29,7 @@
     rhs_v, dinv_v, fac, ko, kx, kl,
     share, fshare, part, acc, f1r,
     a, sb, sr, os, r1, s2, rr, sol, fw3,
-    prev, last,
+    spare, prev, last,
     rhs_sem, dinv_sem, fac_sem, fout_sem, sout_sem,
     plane_send, fw3_send, f1_recv, ag_recv, fw3_recv,
     line_send, s1_recv, rs2_recv,
@@ -61,6 +61,16 @@
             return carry
         lax.fori_loop(low, high, step, 0)
 
+    def start_each(low, high, copy):
+        def step(at, carry):
+            copy(at).start()
+            return carry
+        lax.fori_loop(low, high, step, 0, unroll=4 if isinstance(high, int) else 1)
+
+    def wait_bytes(kib, sem):
+        some = spare.at[pl.ds(0, kib * 2)]
+        pltpu.make_async_copy(some, some, sem).wait()
+
     def rows(gy, gx):
         return pl.ds(pl.multiple_of((gy * 4 + gx) * 16, 16), 16)
 
@@ -99,19 +109,19 @@
         return (lax.broadcasted_iota(jnp.int32, (1, W), 1) < sizes_ref[0, level]).astype(F32)
 
     def plane_copy(o, src, dst, send_sem, recv_sem):
-        i, j = rem4(o), lax.div(o, 4)
-        return send(src(rem4(y + j), rem4(x + i)), dst, send_sem.at[o], recv_sem.at[o], device(i, j, 0, 0))
+        i, j = near_first(rem4(15 - o)), near_first(3 - lax.div(o, 4))
+        return send(src(rem4(y + j), rem4(x + i)), dst, send_sem, recv_sem, device(i, j, 0, 0))
 
     def part_copy(level):
         return lambda o: plane_copy(
-            o, lambda gy, gx: part.at[rows(gy, gx)], f1r.at[level, mine], plane_send, f1_recv.at[level])
+            o, lambda gy, gx: part.at[rows(gy, gx)], f1r.at[level, mine], plane_send.at[0], f1_recv.at[level])
 
     def sol_copy(level):
         return lambda o: plane_copy(
-            o, lambda gy, gx: sol.at[level, mine], sol.at[level, mine], plane_send, ag_recv.at[level])
+            o, lambda gy, gx: sol.at[level, mine], sol.at[level, mine], plane_send.at[0], ag_recv.at[level])
 
     def fw3_copy(o):
-        return plane_copy(o, lambda gy, gx: fw3.at[mine], fw3.at[mine], fw3_send, fw3_recv)
+        return plane_copy(o, lambda gy, gx: fw3.at[mine], fw3.at[mine], fw3_send.at[0], fw3_recv.at[0])
 
     def prepare():
         def one(m):
@@ -170,17 +180,11 @@
         m = level + 1
 
         def s1(o):
-            k, n, i = near_first(lax.div(o, 8)), lax.rem(lax.div(o, 4), 2), rem4(o)
-            half = lax.rem(core + n, 2)
-            return send(
-                share.at[level, half], ko.at[slot, me, y, x], line_send.at[o],
-                s1_recv.at[level, core, k, i], device(i * core, i * other, k, n))
-
-        def s1_arrival(k, n, i):
+            k, n, i = near_first(lax.div(o, 8)), lax.rem(lax.div(o, 4), 2), near_first(rem4(o))
             half = lax.rem(core + n, 2)
             return send(
                 share.at[level, half], ko.at[slot, me, y, x], line_send.at[0],
-                s1_recv.at[level, half, k, i], device(0, 0, 0, 1))
+                s1_recv.at[level, k], device(i * core, i * other, k, n))
 
         def evens(ref, zc, at):
             return ref.at[slot, zc, :, at]
@@ -194,7 +198,7 @@
                 src, to = evens(ko, zc, x), device(i, 0, 0, 0)
             else:
                 src, to = odds(ko, zc, y), device(0, i, 0, 0)
-            return send(src, src, axis_send.at[p, k, i], f5_recv.at[level, p, k, i], to)
+            return send(src, src, axis_send.at[0], f5_recv.at[level, k], to)
 
         def f6(p, k, i):
             zc = rem4(z + 4 - k)
@@ -204,10 +208,11 @@
             else:
                 at = rem4(y + 4 - i)
                 src, dst = odds(ko, zc, at), odds(kx, zc, at)
-            return send(src, dst, sib_send.at[p, k, i], f6_recv.at[level, p, k, i], device(0, 0, 0, 1))
-
-        ko[slot, me, y, x] = share[level, core]
-        each(1, 32, lambda o: s1(o).start())
+            return send(src, dst, sib_send.at[0], f6_recv.at[level], device(0, 0, 0, 1))
+
+        own = pltpu.make_async_copy(share.at[level, core], ko.at[slot, me, y, x], s1_recv.at[level, 0])
+        own.start()
+        start_each(1, 32, s1)
 
         @pl.when(level == 0)
         def _():
@@ -215,8 +220,7 @@
 
         def chunk(kk):
             k = near_first(kk)
-            first = jnp.where(kk == 0, 1, 0)
-            each(first, 8, lambda q: s1_arrival(k, lax.div(q, 4), rem4(q)).wait_recv())
+            wait_bytes(64, s1_recv.at[level, k])
 
             def go(v):
                 i = near_first(v)
@@ -229,13 +233,18 @@
 
         each(0, 4, chunk)
 
-        def relay(v):
-            k, i = near_first(lax.div(v, 3)), near_first(1 + lax.rem(v, 3))
-            for p in (0, 1):
-                f5(p, k, i).wait_recv()
-                f6(p, k, i).start()
-
-        each(0, 12, relay)
+        def relay(kk):
+            k = near_first(kk)
+            wait_bytes(192, f5_recv.at[level, k])
+
+            def go(v):
+                i = near_first(v)
+                f6(0, k, i).start()
+                f6(1, k, i).start()
+
+            each(1, 4, go)
+
+        each(0, 4, relay)
 
         def keep_own(u):
             kl[0, level * 8 + u] = ko[slot, u].reshape(H, H)
@@ -250,34 +259,23 @@
         def half_pass(which):
             @pl.when(which == 1)
             def _():
-                def arrival(v):
-                    for p in (0, 1):
-                        f6(p, lax.div(v, 4), rem4(v)).wait_recv()
-                each(0, 16, arrival)
+                pltpu.make_async_copy(kx.at[slot], kx.at[slot], f6_recv.at[level]).wait()
                 each(0, 8, keep_other)
             accumulate(m, which, lax.rem(core + which, 2))
 
         each(0, 2, half_pass)
         part[...] = acc[...].astype(BF)
-        each(1, 16, lambda o: part_copy(level)(o).start())
+        start_each(0, 15, part_copy(level))
         f1r[level, mine] = part[mine]
         for which in (0, 1):
             forward_out(level, which).start()
-        each(1, 32, lambda o: s1(o).wait_send())
-
-        def sent(v):
-            for p in (0, 1):
-                f5(p, lax.div(v, 3), 1 + lax.rem(v, 3)).wait_send()
-
-        def passed(v):
-            for p in (0, 1):
-                f6(p, lax.div(v, 4), rem4(v)).wait_send()
-
-        each(0, 12, sent)
-        each(0, 16, passed)
+        wait_bytes(248, line_send.at[0])
+        each(0, 4, lambda v: wait_bytes(192, axis_send.at[0]))
+        pltpu.make_async_copy(ko.at[slot], ko.at[slot], sib_send.at[0]).wait()
         rhs_load(m).wait()
         dinv_load(m).wait()
-        each(1, 16, lambda o: part_copy(level)(o).wait())
+        wait_bytes(240, f1_recv.at[level])
+        wait_bytes(240, plane_send.at[0])
         total = jnp.sum(f1r[level].astype(F32).reshape(16, 16, W), axis=0)
         solve_forward(m, (rhs_v[m].astype(F32) - total).astype(BF))
 
@@ -295,8 +293,9 @@
         return pltpu.make_async_copy(sol.at[level], solution_ref.at[level], sout_sem.at[level])
 
     def gather_plane(level):
-        each(1, 16, lambda o: sol_copy(level)(o).start())
-        each(1, 16, lambda o: sol_copy(level)(o).wait())
+        start_each(0, 15, sol_copy(level))
+        wait_bytes(240, ag_recv.at[level])
+        wait_bytes(240, plane_send.at[0])
         solution_out(level).start()
 
     def backward_level(it):
@@ -306,7 +305,7 @@
 
         @pl.when(it == 0)
         def _():
-            each(1, 16, lambda o: fw3_copy(o).start())
+            start_each(0, 15, fw3_copy)
 
         def gathered(unit, which):
             value = a[which, 0, last[0, low * 8 + unit]]
@@ -315,7 +314,7 @@
             return value
 
         def pair(unit):
-            return send(sb.at[unit], sr.at[unit], sib_send.at[lax.div(unit, 4), rem4(unit), 0],
+            return send(sb.at[unit], sr.at[unit], sib_send.at[0],
                         sib_recv.at[low, unit], device(0, 0, 0, 1))
 
         def far_first(kk):
@@ -349,40 +348,33 @@
                 src, to = os.at[zc, :, rem4(x + i)], device(i, 0, 0, 0)
             else:
                 src, to = os.at[4 + zc, rem4(y + i)], device(0, i, 0, 0)
-            return send(src, r1.at[p, i - 1, zc], axis_send.at[p, k, i], rs1_recv.at[low, p, k, i], to)
+            return send(src, r1.at[p, i - 1, zc], axis_send.at[0], rs1_recv.at[low, p, k], to)
 
         def merge(kk):
             k = far_first(kk)
             zc = rem4(z + k)
             for p in (0, 1):
                 unit = p * 4 + zc
-                pair(unit).wait()
+                pair(unit).wait_recv()
                 both = gathered(unit, 1) + sr[unit].reshape(H, H).astype(F32)
                 os[unit] = both.astype(BF).reshape(4, 4, 16, H)
-                each(1, 4, lambda v: rs1(p, k, v).start())
+                start_each(1, 4, lambda v: rs1(p, k, v))
 
         each(0, 4, merge)
 
         def rs2(o):
-            k, n, i = lax.div(o, 8), lax.rem(lax.div(o, 4), 2), rem4(o)
+            k, n, i = lax.div(o, 8), lax.rem(lax.div(o, 4), 2), near_first(rem4(o))
             to = lax.rem(core + n, 2)
             at = rem4(x * to + y * (1 - to) + i)
             return send(
-                s2.at[to, rem4(z + k), at], rr.at[low, core, k, i], line_send.at[o],
-                rs2_recv.at[low, core, k, i], device(i * to, i * (1 - to), k, n))
-
-        def rs2_arrival(o):
-            k, n, i = lax.div(o, 8), lax.rem(lax.div(o, 4), 2), rem4(o)
-            half = lax.rem(core + n, 2)
-            return send(
-                s2.at[0, 0, 0], rr.at[low, half, k, i], line_send.at[0],
-                rs2_recv.at[low, half, k, i], device(0, 0, 0, 1))
+                s2.at[to, rem4(z + k), at], rr.at[low, core, k, i], line_send.at[0],
+                rs2_recv.at[low], device(i * to, i * (1 - to), k, n))
 
         def fold(kk):
             k = far_first(kk)
             zc = rem4(z + k)
             for p in (0, 1):
-                each(1, 4, lambda v: rs1(p, k, v).wait())
+                wait_bytes(96, rs1_recv.at[low, p, k])
                 value = os[zc, :, x] if p == 0 else os[4 + zc, y]
                 value = value.astype(F32)
                 for i in range(3):
@@ -393,8 +385,10 @@
 
         each(0, 4, fold)
         rr[low, core, 0, 0] = s2[core, z, line]
-        each(1, 32, lambda o: rs2(o).wait_send())
-        each(1, 32, lambda o: rs2_arrival(o).wait_recv())
+        pltpu.make_async_copy(sb, sb, sib_send.at[0]).wait()
+        each(0, 4, lambda v: wait_bytes(192, axis_send.at[0]))
+        wait_bytes(248, rs2_recv.at[low])
+        wait_bytes(248, line_send.at[0])
         sums = [jnp.sum(rr[low, half].astype(F32).reshape(16, 16, H), axis=0) for half in range(2)]
         total = jnp.concatenate(sums, axis=1)
         solve_backward(low, (fshare[low].astype(F32) - total).astype(BF))
@@ -403,7 +397,8 @@
     solve_backward(LEV - 1, fshare[LEV - 1])
     each(0, LEV - 1, backward_level)
     gather_plane(0)
-    each(1, 16, lambda o: fw3_copy(o).wait())
+    wait_bytes(240, fw3_recv.at[0])
+    wait_bytes(240, fw3_send.at[0])
     fw3_out = pltpu.make_async_copy(fw3, forward_ref.at[LEV - 1], fout_sem.at[LEV - 1, 0])
     fw3_out.start()
     each(0, LEV, lambda level: solution_out(level).wait())
@@ -443,13 +438,14 @@
             pltpu.VMEM((LEV - 1, 2, 4, 4, 16, H), BF),
             pltpu.VMEM((LEV, H, W), BF),
             pltpu.VMEM((H, W), BF),
+            pltpu.VMEM((W, 128), F32),
             pltpu.SMEM((LEV - 1, SPD), jnp.int32),
             pltpu.SMEM((LEV - 1, 24), jnp.int32),
             dma((LEV,)), dma((LEV,)), dma((LEV - 1,)), dma((LEV, 2)), dma((LEV,)),
-            dma((16,)), dma((16,)), dma((LEV - 1, 16)), dma((LEV, 16)), dma((16,)),
-            dma((32,)), dma((LEV - 1, 2, 4, 4)), dma((LEV - 1, 2, 4, 4)),
-            dma((2, 4, 4)), dma((LEV - 1, 2, 4, 4)), dma((LEV - 1, 2, 4, 4)),
-            dma((2, 4, 4)), dma((LEV - 1, 2, 4, 4)), dma((LEV - 1, 8)),
+            dma((1,)), dma((1,)), dma((LEV - 1,)), dma((LEV,)), dma((1,)),
+            dma((1,)), dma((LEV - 1, 4)), dma((LEV - 1,)),
+            dma((1,)), dma((LEV - 1, 4)), dma((LEV - 1, 2, 4)),
+            dma((1,)), dma((LEV - 1,)), dma((LEV - 1, 8)),
         ],
         compiler_params=pltpu.CompilerParams(
             collective_id=0, has_side_effects=True, vmem_limit_bytes=61 << 20),

time: 161 us -> 150 us (0.932)
  Pallas kernels: 156 us -> 145 us
    pallas_call x1, Pallas kernels: 156 us -> 145 us  [shards(): pl.pallas_call(kernel, out_shape=[jax.ShapeDtypeStruct((LEV, H, W), BF)]...]
where the time goes in v3:
time: 150 us
  Pallas kernels  145 us (97%)
  local copies, waits for them, and re-layouts  4.52 us (3%)
    pallas_call x1, Pallas kernels, shards(): pl.pallas_call(kernel, out_shape=[jax.ShapeDtypeStruct((LEV, H, W), BF)]...  145 us
    unnamed x2, local copies, waits for them, and re-layouts  4.52 us

profile of v3, /device:TPU:1, one launch (start us, length us, event | category | flops | bytes accessed | tf_op | source)
XLA Modules:
  0.0 150.0 jit_solution(5567722583623148473)
XLA Ops:
  0.6 144.9 %levels.1 = (bf16[4,256,512]{2,1,0:T(8,128)(2,1)}, bf16[4,256,512]{2,1,0:T(8,128)(2,1)}) custom-call(bf16[4,1,256,512]{3,2,1,0:T(8,128)(2,1)} %rhs_ref.1, bf16[4,1,512,512]{3,2,1,0:T(8,128)(2,1)} %dinv_ref.1, bf16[3,1,12,512,512]{4,3,2,1,0:T(8,128)(2,1)} %factor_ref.1, s32[3,1,12]{2,1,0:T(1,128)} %deps_ref.1, s32[1,1,3]{2,1,0:T(1,128)} %bitcast.10, ...), custom_call_target="tpu_custom_call" | custom-call | tf_op jit(solution)/shard_map/levels/pallas_call | solution.py:415
  145.5 2.3 %copy.12 = bf16[4,1,256,512]{3,2,1,0:T(8,128)(2,1)} copy(bf16[4,1,256,512]{3,2,1,0:T(8,128)(2,1)} %bitcast.9) | data formatting | bytes 2097152
  147.8 2.3 %copy.13 = bf16[4,1,256,512]{3,2,1,0:T(8,128)(2,1)} copy(bf16[4,1,256,512]{3,2,1,0:T(8,128)(2,1)} %bitcast.8) | data formatting | bytes 2097152

commit v4 on v0

v4 whole, which is shorter than its diff:
```python
import jax
import jax.numpy as jnp
from jax import lax
from jax.experimental import pallas as pl
from jax.experimental.pallas import tpu as pltpu
from jax.sharding import PartitionSpec as P

MESH = pl.DeviceIdType.MESH
BF = jnp.bfloat16
F32 = jnp.float32
LEV = 4
SPD = 12
W = 512
H = 256
Q = 128


def rem4(v):
    return lax.rem(v, 4)


def near_first(v):
    return v + lax.div(v, 2) * (5 - 2 * v)


def fold(v):
    n, c = v.shape
    t = v.reshape(n // 8, 8, c)
    return jnp.concatenate([t[:, :, : c // 2], t[:, :, c // 2 :]], axis=1)


def unfold(v):
    n, _, c = v.shape
    return jnp.concatenate([v[:, :8], v[:, 8:]], axis=2).reshape(n * 8, 2 * c)


def kernel(
    rhs_ref, dinv_ref, factor_ref, deps_ref, counts_ref, sizes_ref,
    forward_ref, solution_ref,
    rhs_v, rhs_f, dinv_v, fac, ko, kx, kl,
    share, fshare, part, acc, f1r,
    a, sb, sr, os, r1, s2, rr, solg, sfull, fw3, outs,
    spare, prev, last,
    rhs_sem, dinv_sem, fac_sem, out_sem,
    plane_send, fw3_send, f1_recv, ag_recv, fw3_recv,
    line_send, s1_recv, rs2_recv,
    axis_send, f5_recv, rs1_recv,
    sib_send, f6_recv, sib_recv,
):
    layer, row, col = lax.axis_index("layer"), lax.axis_index("row"), lax.axis_index("col")
    x = rem4(col)
    y = layer * 2 + lax.div(col, 4)
    z = lax.div(row, 2)
    core = lax.rem(row, 2)
    other = 1 - core
    me = core * 4 + z
    line = x * core + y * other

    def device(i, j, k, n):
        xx, yy, zz, cc = rem4(x + i), rem4(y + j), rem4(z + k), lax.rem(core + n, 2)
        return (lax.div(yy, 2), zz * 2 + cc, lax.rem(yy, 2) * 4 + xx)

    def send(src, dst, send_sem, recv_sem, to):
        return pltpu.make_async_remote_copy(
            src_ref=src, dst_ref=dst, send_sem=send_sem, recv_sem=recv_sem,
            device_id=to, device_id_type=MESH,
        )

    def each(low, high, body):
        def step(at, carry):
            body(at)
            return carry
        lax.fori_loop(low, high, step, 0)

    def start_each(low, high, copy):
        def step(at, carry):
            copy(at).start()
            return carry
        lax.fori_loop(low, high, step, 0, unroll=4 if isinstance(low, int) else None)

    def wait_bytes(kib, sem):
        some = spare.at[pl.ds(0, kib * 2)]
        pltpu.make_async_copy(some, some, sem).wait()

    def half_cols(half):
        return pl.ds(pl.multiple_of(half * H, H), H)

    barrier = pltpu.get_barrier_semaphore()

    def greet(i, j, k, n):
        pl.semaphore_signal(barrier, inc=1, device_id=device(i, j, k, n), device_id_type=MESH)

    def rhs_load(level):
        mine = pl.ds(pl.multiple_of((y * 4 + x) * 16, 16), 16)
        return pltpu.make_async_copy(rhs_ref.at[level, 0, mine], rhs_v.at[level], rhs_sem.at[level])

    def dinv_load(level):
        return pltpu.make_async_copy(dinv_ref.at[level, 0], dinv_v.at[level], dinv_sem.at[level])

    def fac_load(m):
        return pltpu.make_async_copy(factor_ref.at[m, 0], fac.at[m], fac_sem.at[m])

    def start_loads(level):
        rhs_load(level).start()
        dinv_load(level).start()

    start_loads(0)
    each(1, 16, lambda o: greet(rem4(o), lax.div(o, 4), 0, 0))
    each(4, 32, lambda o: greet(0, rem4(o), lax.div(o, 8), lax.rem(lax.div(o, 4), 2)))
    each(3, 24, lambda o: greet(
        1 + lax.rem(o, 3), 0, lax.div(o, 6), lax.rem(lax.div(o, 3), 2)))
    each(1, LEV, start_loads)
    each(0, LEV - 1, lambda m: fac_load(m).start())

    def live_rows(level):
        return (lax.broadcasted_iota(jnp.int32, (1, W), 1) < sizes_ref[0, level]).astype(F32)

    def plane_copy(o, src, dst, send_sem, recv_sem):
        i, j = near_first(rem4(15 - o)), near_first(3 - lax.div(o, 4))
        return send(src(rem4(y + j), rem4(x + i)), dst, send_sem, recv_sem, device(i, j, 0, 0))

    def part_copy(level, h):
        return lambda o: plane_copy(
            o, lambda gy, gx: part.at[h, gy, gx], f1r.at[level, h, y, x],
            plane_send.at[h], f1_recv.at[level, h])

    def sol_copy(level, h):
        return lambda o: plane_copy(
            o, lambda gy, gx: solg.at[level, h, y, x], solg.at[level, h, y, x],
            plane_send.at[h], ag_recv.at[level, h])

    def fw3_copy(h):
        return lambda o: plane_copy(
            o, lambda gy, gx: fw3.at[h, y, x], fw3.at[h, y, x], fw3_send.at[h], fw3_recv.at[h])

    def prepare(m):
        count = counts_ref[0, 0, m]
        keys = [jnp.where(k < count, deps_ref[m, 0, k], 255) for k in range(SPD)]
        for k in range(SPD):
            at = jnp.int32(SPD)
            for j in range(k):
                at = jnp.where(keys[j] == keys[k], j, at)
            prev[m, k] = at

        def target(t):
            unit = lax.rem(t, 8)
            name = lax.div(t, 8) * 8 + rem4(unit) * 2 + lax.div(unit, 4)
            at = jnp.int32(SPD)
            for k in range(SPD):
                at = jnp.where(keys[k] == name, k, at)
            last[m, t] = at

        each(0, 24, target)
        for h in (0, 1):
            for which in (0, 1):
                a[h, which, m, SPD] = jnp.zeros((Q, H), F32)

    def solve_forward(level, h, resid):
        product = lax.dot_general(
            resid, dinv_v[level], (((1,), (1,)), ((), ())), preferred_element_type=F32)
        solved = (product * live_rows(level)).astype(BF).astype(F32)
        fshare[level, h] = solved
        share[level, h, 0] = fold(solved[:, :H])[0].astype(BF)
        share[level, h, 1] = fold(solved[:, H:])[0].astype(BF)

    def solve_backward(level, h, resid):
        product = jnp.dot(resid, dinv_v[level], preferred_element_type=F32)
        solg[level, h, y, x] = fold(product * live_rows(level))[0].astype(BF)
        start_each(0, 15, sol_copy(level, h))

    def gather_start(level, h):
        def s1(o):
            k, n, i = near_first(lax.div(o, 8)), lax.rem(lax.div(o, 4), 2), near_first(rem4(o))
            half = lax.rem(core + n, 2)
            return send(
                share.at[level, h, half], ko.at[lax.rem(level, 2), h, me, y, x], line_send.at[h],
                s1_recv.at[level, h, k], device(i * core, i * other, k, n))

        pltpu.make_async_copy(
            share.at[level, h, core], ko.at[lax.rem(level, 2), h, me, y, x],
            s1_recv.at[level, h, 0]).start()
        start_each(1, 32, s1)

    def result_out(at, ref, level):
        return pltpu.make_async_copy(outs.at[at, level], ref.at[level], out_sem.at[at, level])

    def rows_of_both(parts):
        both = [v.reshape(16, 8, v.shape[-1]) for v in parts]
        return jnp.concatenate(both, axis=1).astype(BF).reshape(H, both[0].shape[-1])

    def forward_level(level):
        slot = lax.rem(level, 2)
        m = level + 1

        def evens(ref, h, zc, at):
            return ref.at[slot, h, zc, :, at]

        def odds(ref, h, zc, at):
            return ref.at[slot, h, 4 + zc, at]

        def f5(h, p, k, i):
            zc = rem4(z + 4 - k)
            if p == 0:
                src, to = evens(ko, h, zc, x), device(i, 0, 0, 0)
            else:
                src, to = odds(ko, h, zc, y), device(0, i, 0, 0)
            return send(src, src, axis_send.at[h], f5_recv.at[level, h, k], to)

        def f6(h, p, k, i):
            zc = rem4(z + 4 - k)
            if p == 0:
                at = rem4(x + 4 - i)
                src, dst = evens(ko, h, zc, at), evens(kx, h, zc, at)
            else:
                at = rem4(y + 4 - i)
                src, dst = odds(ko, h, zc, at), odds(kx, h, zc, at)
            return send(src, dst, sib_send.at[h], f6_recv.at[level, h], device(0, 0, 0, 1))

        def spread(h):
            def chunk(kk):
                k = near_first(kk)
                wait_bytes(32, s1_recv.at[level, h, k])

                def go(v):
                    i = near_first(v)
                    f5(h, 0, k, i).start()
                    f5(h, 1, k, i).start()

                each(1, 4, go)
                f6(h, 0, k, 0).start()
                f6(h, 1, k, 0).start()

            each(0, 4, chunk)

        each(0, 2, spread)

        def finish(h):
            def relay(kk):
                k = near_first(kk)
                wait_bytes(96, f5_recv.at[level, h, k])

                def go(v):
                    i = near_first(v)
                    f6(h, 0, k, i).start()
                    f6(h, 1, k, i).start()

                each(1, 4, go)

            each(0, 4, relay)

            @pl.when(h == 0)
            def _():
                fac_load(level).wait()

            acc[...] = jnp.zeros_like(acc)

            def half_pass(which):
                @pl.when(which == 0)
                def _():
                    def keep(u):
                        kl[h, 0, level * 8 + u] = unfold(
                            ko[slot, h, u].astype(F32).reshape(16, 16, Q)).astype(BF)
                    each(0, 8, keep)

                @pl.when(which == 1)
                def _():
                    pltpu.make_async_copy(kx.at[slot, h], kx.at[slot, h], f6_recv.at[level, h]).wait()

                    def keep(u):
                        kl[h, 1, level * 8 + u] = unfold(
                            kx[slot, h, u].astype(F32).reshape(16, 16, Q)).astype(BF)
                    each(0, 8, keep)

                half = lax.rem(core + which, 2)

                def add(k, carry):
                    dep = deps_ref[level, 0, k]
                    r = lax.rem(dep, 8)
                    at = dep - r + lax.rem(r, 2) * 4 + lax.div(r, 2)
                    value = kl[h, which, at]
                    value = jnp.where(k < counts_ref[0, 0, level], value, jnp.zeros_like(value))
                    block = fac[level, k, :, half_cols(half)]
                    acc[...] += lax.dot_general(
                        value, block, (((1,), (1,)), ((), ())), preferred_element_type=F32)
                    return carry

                lax.fori_loop(0, SPD, add, 0, unroll=True)

            each(0, 2, half_pass)
            part[h] = fold(acc[...]).astype(BF).reshape(4, 4, 16, H)
            start_each(0, 15, part_copy(level, h))
            f1r[level, h, y, x] = part[h, y, x]
            wait_bytes(124, line_send.at[h])
            wait_bytes(192, axis_send.at[h])
            wait_bytes(192, axis_send.at[h])
            pltpu.make_async_copy(ko.at[slot, h], ko.at[slot, h], sib_send.at[h]).wait()

        each(0, 2, finish)
        for half in (0, 1):
            which = lax.rem(core + half, 2)
            outs[0, level, :, half * H : (half + 1) * H] = rows_of_both(
                [kl[h, which, level * 8 + me].astype(F32) for h in (0, 1)])
        result_out(0, forward_ref, level).start()
        dinv_load(m).wait()

        def next_level(h):
            wait_bytes(120, f1_recv.at[level, h])
            wait_bytes(120, plane_send.at[h])
            total = unfold(jnp.sum(
                f1r[level, h].astype(F32).reshape(16, 16, H), axis=0, keepdims=True))
            solve_forward(m, h, (rhs_f[m, h] - total).astype(BF))

            @pl.when(level < LEV - 2)
            def _():
                gather_start(m, h)

            @pl.when(level == LEV - 2)
            def _():
                fw3[h, y, x] = fold(fshare[LEV - 1, h])[0].astype(BF)
                solve_backward(LEV - 1, h, fshare[LEV - 1, h].astype(BF))

        each(0, 2, next_level)

    rhs_load(0).wait()

    def split_rhs(level):
        both = rhs_v[level].astype(F32)
        rhs_f[level, 0] = both[:8]
        rhs_f[level, 1] = both[8:]

    split_rhs(0)
    dinv_load(0).wait()
    each(0, 2, lambda h: solve_forward(0, h, rhs_f[0, h].astype(BF)))
    pl.semaphore_wait(barrier, 64)
    each(0, 2, lambda h: gather_start(0, h))

    def late(level):
        rhs_load(level).wait()
        split_rhs(level)

    each(1, LEV, late)
    each(0, LEV - 1, prepare)
    each(0, LEV - 1, forward_level)

    def take_plane(level, h):
        wait_bytes(120, ag_recv.at[level, h])
        wait_bytes(120, plane_send.at[h])

    def plane_result(at, ref, level, parts):
        outs[at, level] = rows_of_both([unfold(v.astype(F32).reshape(16, 16, H)) for v in parts])
        result_out(at, ref, level).start()

    def backward_level(it):
        level = LEV - 1 - it
        low = level - 1

        def far_first(kk):
            return near_first(3 - kk)

        def gathered(h, unit, which):
            value = a[h, which, 0, last[0, low * 8 + unit]]
            for m in range(1, LEV - 1):
                value = value + a[h, which, m, last[m, low * 8 + unit]]
            return fold(value)

        def pair(h, unit):
            return send(sb.at[h, unit], sr.at[h, unit], sib_send.at[h],
                        sib_recv.at[low, h, unit], device(0, 0, 0, 1))

        def rs1(h, p, k, i):
            zc = rem4(z + k)
            if p == 0:
                src, to = os.at[h, zc, :, rem4(x + i)], device(i, 0, 0, 0)
            else:
                src, to = os.at[h, 4 + zc, rem4(y + i)], device(0, i, 0, 0)
            return send(src, r1.at[h, p, i - 1, zc], axis_send.at[h], rs1_recv.at[low, h, p, k], to)

        def rs2(h, o):
            k, n, i = lax.div(o, 8), lax.rem(lax.div(o, 4), 2), near_first(rem4(o))
            to = lax.rem(core + n, 2)
            at = rem4(x * to + y * (1 - to) + i)
            return send(
                s2.at[h, to, rem4(z + k), at], rr.at[low, h, core, k, i], line_send.at[h],
                rs2_recv.at[low, h], device(i * to, i * (1 - to), k, n))

        def terms(h):
            take_plane(level, h)
            sfull[h] = unfold(solg[level, h].astype(F32).reshape(16, 16, H)).astype(BF)

            def to_sibling(q):
                unit = lax.rem(q, 2) * 4 + rem4(z + far_first(lax.div(q, 2)))
                sb[h, unit] = gathered(h, unit, 0).astype(BF).reshape(4, 4, 16, Q)
                pair(h, unit).start()

            def contributions(which):
                half = lax.rem(core + 1 + which, 2)

                def slot(k, carry):
                    block = fac[low, k, :, half_cols(half)]
                    term = jnp.dot(sfull[h], block, preferred_element_type=F32)
                    a[h, which, low, k] = term + a[h, which, low, prev[low, k]]
                    return carry

                lax.fori_loop(0, SPD, slot, 0, unroll=True)

                @pl.when(which == 0)
                def _():
                    each(0, 8, to_sibling)

            each(0, 2, contributions)

            def merge(kk):
                k = far_first(kk)
                zc = rem4(z + k)
                for p in (0, 1):
                    unit = p * 4 + zc
                    pair(h, unit).wait_recv()
                    both = gathered(h, unit, 1) + sr[h, unit].astype(F32).reshape(16, 16, Q)
                    os[h, unit] = both.astype(BF).reshape(4, 4, 16, Q)
                    start_each(1, 4, lambda v: rs1(h, p, k, v))

            each(0, 4, merge)

        each(0, 2, terms)

        @pl.when(it == 0)
        def _():
            each(0, 2, lambda h: start_each(0, 15, fw3_copy(h)))

        plane_result(1, solution_ref, level, [solg[level, h] for h in (0, 1)])

        def fold_axis(h):
            def chunk(kk):
                k = far_first(kk)
                zc = rem4(z + k)
                for p in (0, 1):
                    wait_bytes(48, rs1_recv.at[low, h, p, k])
                    value = os[h, zc, :, x] if p == 0 else os[h, 4 + zc, y]
                    value = value.astype(F32)
                    for i in range(3):
                        value = value + r1[h, p, i, zc].astype(F32)
                    s2[h, p, zc] = value.astype(BF)
                first = jnp.where(kk == 3, 1, 0)
                start_each(first, 8, lambda q: rs2(h, k * 8 + q))

            each(0, 4, chunk)
            rr[low, h, core, 0, 0] = s2[h, core, z, line]

        each(0, 2, fold_axis)

        def solve(h):
            wait_bytes(124, rs2_recv.at[low, h])
            sums = [
                unfold(jnp.sum(
                    rr[low, h, half].astype(F32).reshape(16, 16, Q), axis=0, keepdims=True))
                for half in range(2)]
            total = jnp.concatenate(sums, axis=1)
            solve_backward(low, h, (fshare[low, h] - total).astype(BF))
            wait_bytes(124, line_send.at[h])
            wait_bytes(192, axis_send.at[h])
            wait_bytes(192, axis_send.at[h])
            pltpu.make_async_copy(sb.at[h], sb.at[h], sib_send.at[h]).wait()

        each(0, 2, solve)

    each(0, LEV - 1, backward_level)
    for h in (0, 1):
        wait_bytes(120, fw3_recv.at[h])
        wait_bytes(120, fw3_send.at[h])
    plane_result(0, forward_ref, LEV - 1, [fw3[h] for h in (0, 1)])
    each(0, 2, lambda h: take_plane(0, h))
    plane_result(1, solution_ref, 0, [solg[0, h] for h in (0, 1)])
    each(0, LEV, lambda level: result_out(0, forward_ref, level).wait())
    each(0, LEV, lambda level: result_out(1, solution_ref, level).wait())


def shards(rhs, dinv, factor, deps, counts, sizes):
    any_spec = pl.BlockSpec(memory_space=pl.ANY)
    smem = pl.BlockSpec(memory_space=pltpu.SMEM)
    dma = pltpu.SemaphoreType.DMA
    block = (2, 8, 4, 4, 16, Q)
    forward, solved = pl.pallas_call(
        kernel,
        out_shape=[jax.ShapeDtypeStruct((LEV, H, W), BF)] * 2,
        in_specs=[any_spec] * 3 + [smem] * 3,
        out_specs=[any_spec] * 2,
        scratch_shapes=[
            pltpu.VMEM((LEV, 16, W), BF),
            pltpu.VMEM((LEV, 2, 8, W), F32),
            pltpu.VMEM((LEV, W, W), BF),
            pltpu.VMEM((LEV - 1, SPD, W, W), BF),
            pltpu.VMEM((2,) + block, BF),
            pltpu.VMEM((2,) + block, BF),
            pltpu.VMEM((2, 2, 24, Q, H), BF),
            pltpu.VMEM((LEV, 2, 2, 16, Q), BF),
            pltpu.VMEM((LEV, 2, 8, W), F32),
            pltpu.VMEM((2, 4, 4, 16, H), BF),
            pltpu.VMEM((Q, W), F32),
            pltpu.VMEM((LEV - 1, 2, 4, 4, 16, H), BF),
            pltpu.VMEM((2, 2, LEV - 1, SPD + 1, Q, H), F32),
            pltpu.VMEM(block, BF),
            pltpu.VMEM(block, BF),
            pltpu.VMEM(block, BF),
            pltpu.VMEM((2, 2, 3, 4, 4, 16, Q), BF),
            pltpu.VMEM((2, 2, 4, 4, 16, Q), BF),
            pltpu.VMEM((LEV - 1, 2, 2, 4, 4, 16, Q), BF),
            pltpu.VMEM((LEV, 2, 4, 4, 16, H), BF),
            pltpu.VMEM((2, Q, W), BF),
            pltpu.VMEM((2, 4, 4, 16, H), BF),
            pltpu.VMEM((2, LEV, H, W), BF),
            pltpu.VMEM((W, 128), F32),
            pltpu.SMEM((LEV - 1, SPD), jnp.int32),
            pltpu.SMEM((LEV - 1, 24), jnp.int32),
            dma((LEV,)), dma((LEV,)), dma((LEV - 1,)), dma((2, LEV)),
            dma((2,)), dma((2,)), dma((LEV - 1, 2)), dma((LEV, 2)), dma((2,)),
            dma((2,)), dma((LEV - 1, 2, 4)), dma((LEV - 1, 2)),
            dma((2,)), dma((LEV - 1, 2, 4)), dma((LEV - 1, 2, 2, 4)),
            dma((2,)), dma((LEV - 1, 2)), dma((LEV - 1, 2, 8)),
        ],
        compiler_params=pltpu.CompilerParams(
            collective_id=0, has_side_effects=True, vmem_limit_bytes=61 << 20),
        name="levels",
    )(rhs, dinv, factor, deps, counts.transpose(1, 2, 0), sizes.T)
    return forward[:, None], solved[:, None]


def solution(mesh):
    placed = (
        P(None, "row", None, None),
        P(None, "row", None, None),
        P(None, "row", ("layer", "col"), None, None),
        P(None, "row", ("layer", "col")),
        P(None, "row", ("layer", "col")),
        P(None, "row"),
    )
    return jax.shard_map(
        shards,
        mesh=mesh,
        in_specs=placed,
        out_specs=(P(None, "row", None, None), P(None, "row", None, None)),
        check_vma=False,
    )
```

time: 2490 us -> 134 us (0.05); the launches traced: 2460 us -> 133 us
  waiting for transfers between devices: 2240 us -> 0 us
  Pallas kernels: 0 us -> 128 us
  other arithmetic: 61.9 us -> 0 us
  matrix products: 52.4 us -> 0 us
  blocking collectives: 47.7 us -> 0 us
  local copies, waits for them, and re-layouts: 43.2 us -> 4.52 us
    reduce_scatter x3 -> x0, waiting for transfers between devices: 1920 us -> none  [shards(): lax.psum_scatter(arranged, ('layer', 'row', 'col'), scatter_dimension=0,...]
    psum x3 -> x0, waiting for transfers between devices: 249 us -> none  [shards(): total = lax.psum(partial_value, ('layer', 'col'))]
    pallas_call x0 -> x1, Pallas kernels: none -> 128 us  [shards(): pl.pallas_call(kernel, out_shape=[jax.ShapeDtypeStruct((LEV, H, W), BF)]...]
    all_gather x3 -> x0, waiting for transfers between devices: 77.7 us -> none  [shards(): stash.append(lax.all_gather(solved[None], 'row', axis=0, tiled=True))]
    dot_general x14 -> x0, matrix products: 52.4 us -> none  [the longest x3 21.8 us: shards(): jnp.einsum('nj,kji->kni', solved, factor[level - 1, 0], preferred_element...]
    all_gather x3 -> x0, blocking collectives: 47.7 us -> none  [shards(): solved = lax.all_gather(piece, ('layer', 'col'), axis=0, tiled=True)]
    scatter-add x3 -> x0, other arithmetic: 41 us -> none  [shards(): carried = carried.at[deps[level - 1, 0]].add(terms)]
  transfers between devices with their start and end apart: 9 -> 0, of which waited for: 9 -> 0; matrix products, arithmetic and copies ran while one was open for 0% -> 0% of each run, Pallas kernels for 0% -> 0%
where the time goes in v4:
time: 134 us; the launch traced here: 133 us
  Pallas kernels  128 us (96%)
  local copies, waits for them, and re-layouts  4.52 us (3%)
    pallas_call x1, Pallas kernels, shards(): pl.pallas_call(kernel, out_shape=[jax.ShapeDtypeStruct((LEV, H, W), BF)]...  128 us
    unnamed x2, local copies, waits for them, and re-layouts  4.52 us

profile of v4, /device:TPU:1, one launch (start us, length us, event | category | flops | bytes accessed | tf_op | source)
XLA Modules:
  0.0 133.4 jit_solution(15554377090081096720)
XLA Ops:
  0.6 128.3 %levels.1 = (bf16[4,256,512]{2,1,0:T(8,128)(2,1)}, bf16[4,256,512]{2,1,0:T(8,128)(2,1)}) custom-call(bf16[4,1,256,512]{3,2,1,0:T(8,128)(2,1)} %rhs_ref.1, bf16[4,1,512,512]{3,2,1,0:T(8,128)(2,1)} %dinv_ref.1, bf16[3,1,12,512,512]{4,3,2,1,0:T(8,128)(2,1)} %factor_ref.1, s32[3,1,12]{2,1,0:T(1,128)} %deps_ref.1, s32[1,1,3]{2,1,0:T(1,128)} %bitcast.10, ...), custom_call_target="tpu_custom_call" | custom-call | tf_op jit(solution)/shard_map/levels/pallas_call | solution.py:482
  128.9 2.3 %copy.12 = bf16[4,1,256,512]{3,2,1,0:T(8,128)(2,1)} copy(bf16[4,1,256,512]{3,2,1,0:T(8,128)(2,1)} %bitcast.9) | data formatting | bytes 2097152
  131.2 2.3 %copy.13 = bf16[4,1,256,512]{3,2,1,0:T(8,128)(2,1)} copy(bf16[4,1,256,512]{3,2,1,0:T(8,128)(2,1)} %bitcast.8) | data formatting | bytes 2097152

commit v5 on v4

--- a/solution.py
+++ b/solution.py
@@ -76,7 +76,7 @@
         def step(at, carry):
             copy(at).start()
             return carry
-        lax.fori_loop(low, high, step, 0, unroll=4 if isinstance(low, int) else None)
+        lax.fori_loop(low, high, step, 0, unroll=True)
 
     def wait_bytes(kib, sem):
         some = spare.at[pl.ds(0, kib * 2)]
@@ -105,10 +105,12 @@
         dinv_load(level).start()
 
     start_loads(0)
-    each(1, 16, lambda o: greet(rem4(o), lax.div(o, 4), 0, 0))
-    each(4, 32, lambda o: greet(0, rem4(o), lax.div(o, 8), lax.rem(lax.div(o, 4), 2)))
-    each(3, 24, lambda o: greet(
-        1 + lax.rem(o, 3), 0, lax.div(o, 6), lax.rem(lax.div(o, 3), 2)))
+    for o in range(1, 16):
+        greet(o % 4, o // 4, 0, 0)
+    for o in range(4, 32):
+        greet(0, o % 4, o // 8, o // 4 % 2)
+    for o in range(3, 24):
+        greet(1 + o % 3, 0, o // 6, o // 3 % 2)
     each(1, LEV, start_loads)
     each(0, LEV - 1, lambda m: fac_load(m).start())
 
@@ -221,12 +223,9 @@
                 k = near_first(kk)
                 wait_bytes(32, s1_recv.at[level, h, k])
 
-                def go(v):
-                    i = near_first(v)
+                for i in (2, 1, 3):
                     f5(h, 0, k, i).start()
                     f5(h, 1, k, i).start()
-
-                each(1, 4, go)
                 f6(h, 0, k, 0).start()
                 f6(h, 1, k, 0).start()
 
@@ -239,12 +238,9 @@
                 k = near_first(kk)
                 wait_bytes(96, f5_recv.at[level, h, k])
 
-                def go(v):
-                    i = near_first(v)
+                for i in (1, 3, 2):
                     f6(h, 0, k, i).start()
                     f6(h, 1, k, i).start()
-
-                each(1, 4, go)
 
             each(0, 4, relay)
 
@@ -417,17 +413,12 @@
                     pair(h, unit).wait_recv()
                     both = gathered(h, unit, 1) + sr[h, unit].astype(F32).reshape(16, 16, Q)
                     os[h, unit] = both.astype(BF).reshape(4, 4, 16, Q)
-                    start_each(1, 4, lambda v: rs1(h, p, k, v))
+                    for i in (2, 1, 3):
+                        rs1(h, p, k, i).start()
 
             each(0, 4, merge)
 
         each(0, 2, terms)
-
-        @pl.when(it == 0)
-        def _():
-            each(0, 2, lambda h: start_each(0, 15, fw3_copy(h)))
-
-        plane_result(1, solution_ref, level, [solg[level, h] for h in (0, 1)])
 
         def fold_axis(h):
             def chunk(kk):
@@ -440,8 +431,8 @@
                     for i in range(3):
                         value = value + r1[h, p, i, zc].astype(F32)
                     s2[h, p, zc] = value.astype(BF)
-                first = jnp.where(kk == 3, 1, 0)
-                start_each(first, 8, lambda q: rs2(h, k * 8 + q))
+                pl.when(kk < 3)(lambda: rs2(h, k * 8).start())
+                start_each(1, 8, lambda q: rs2(h, k * 8 + q))
 
             each(0, 4, chunk)
             rr[low, h, core, 0, 0] = s2[h, core, z, line]
@@ -462,6 +453,11 @@
             pltpu.make_async_copy(sb.at[h], sb.at[h], sib_send.at[h]).wait()
 
         each(0, 2, solve)
+        plane_result(1, solution_ref, level, [solg[level, h] for h in (0, 1)])
+
+        @pl.when(it == 0)
+        def _():
+            each(0, 2, lambda h: start_each(0, 15, fw3_copy(h)))
 
     each(0, LEV - 1, backward_level)
     for h in (0, 1):
@@ -472,6 +468,32 @@
     plane_result(1, solution_ref, 0, [solg[0, h] for h in (0, 1)])
     each(0, LEV, lambda level: result_out(0, forward_ref, level).wait())
     each(0, LEV, lambda level: result_out(1, solution_ref, level).wait())
+
+
+def result_kernel(a_in, b_in, a_out, b_out, held, in_sem, out_sem):
+    ways = [(at, src, dst, level) for level in range(LEV)
+            for at, src, dst in ((0, a_in, a_out), (1, b_in, b_out))]
+    for at, src, dst, level in ways:
+        pltpu.make_async_copy(src.at[level], held.at[at, level], in_sem.at[at, level]).start()
+    for at, src, dst, level in ways:
+        pltpu.make_async_copy(src.at[level], held.at[at, level], in_sem.at[at, level]).wait()
+        pltpu.make_async_copy(held.at[at, level], dst.at[level], out_sem.at[at, level]).start()
+    for at, src, dst, level in ways:
+        pltpu.make_async_copy(held.at[at, level], dst.at[level], out_sem.at[at, level]).wait()
+
+
+def results(a, b):
+    any_spec = pl.BlockSpec(memory_space=pl.ANY)
+    sems = pltpu.SemaphoreType.DMA((2, LEV))
+    return pl.pallas_call(
+        result_kernel,
+        out_shape=[jax.ShapeDtypeStruct(a.shape, a.dtype)] * 2,
+        in_specs=[any_spec] * 2,
+        out_specs=[any_spec] * 2,
+        scratch_shapes=[pltpu.VMEM((2,) + a.shape, a.dtype), sems, sems],
+        compiler_params=pltpu.CompilerParams(vmem_limit_bytes=60 << 20),
+        name="results",
+    )(a, b)
 
 
 def shards(rhs, dinv, factor, deps, counts, sizes):
@@ -521,6 +543,7 @@
             collective_id=0, has_side_effects=True, vmem_limit_bytes=61 << 20),
         name="levels",
     )(rhs, dinv, factor, deps, counts.transpose(1, 2, 0), sizes.T)
+    forward, solved = results(forward, solved)
     return forward[:, None], solved[:, None]
 
 

time: 134 us -> 126 us (0.940)
  local copies, waits for them, and re-layouts: 4.52 us -> 0 us
  Pallas kernels: 128 us -> 125 us
    pallas_call x1, Pallas kernels: 128 us -> 123 us  [shards(): pl.pallas_call(kernel, out_shape=[jax.ShapeDtypeStruct((LEV, H, W), BF)]...]
    unnamed x2 -> x0, local copies, waits for them, and re-layouts: 4.52 us -> none
    pallas_call x0 -> x1, Pallas kernels: none -> 2.39 us  [results(): pl.pallas_call(result_kernel, out_shape=[jax.ShapeDtypeStruct(a.shape, a....]
where the time goes in v5:
time: 126 us
  Pallas kernels  125 us (99%)
    pallas_call x1, Pallas kernels, shards(): pl.pallas_call(kernel, out_shape=[jax.ShapeDtypeStruct((LEV, H, W), BF)]...  123 us

profile of v5, /device:TPU:1, one launch (start us, length us, event | category | flops | bytes accessed | tf_op | source)
XLA Modules:
  0.0 126.1 jit_solution(16089499102101674752)
XLA Ops:
  0.6 123.1 %levels.1 = (bf16[4,256,512]{2,1,0:T(8,128)(2,1)}, bf16[4,256,512]{2,1,0:T(8,128)(2,1)}) custom-call(bf16[4,1,256,512]{3,2,1,0:T(8,128)(2,1)} %rhs_ref.1, bf16[4,1,512,512]{3,2,1,0:T(8,128)(2,1)} %dinv_ref.1, bf16[3,1,12,512,512]{4,3,2,1,0:T(8,128)(2,1)} %factor_ref.1, s32[3,1,12]{2,1,0:T(1,128)} %deps_ref.1, s32[1,1,3]{2,1,0:T(1,128)} %bitcast.8, ...), custom_call_target="tpu_custom_call" | custom-call | tf_op jit(solution)/shard_map/levels/pallas_call | solution.py:504
  123.7 2.4 %results.1 = (bf16[4,256,512]{2,1,0:T(8,128)(2,1)}, bf16[4,256,512]{2,1,0:T(8,128)(2,1)}) custom-call(bf16[4,256,512]{2,1,0:T(8,128)(2,1)} %get-tuple-element.6.a_in, bf16[4,256,512]{2,1,0:T(8,128)(2,1)} %get-tuple-element.7.b_in), custom_call_target="tpu_custom_call" | custom-call | tf_op jit(solution)/shard_map/results/pallas_call | solution.py:488

commit v6 on v5

--- a/solution.py
+++ b/solution.py
@@ -190,6 +190,15 @@
         both = [v.reshape(16, 8, v.shape[-1]) for v in parts]
         return jnp.concatenate(both, axis=1).astype(BF).reshape(H, both[0].shape[-1])
 
+    def split_rhs(level):
+        both = rhs_v[level].astype(F32)
+        rhs_f[level, 0] = both[:8]
+        rhs_f[level, 1] = both[8:]
+
+    def late(level):
+        rhs_load(level).wait()
+        split_rhs(level)
+
     def forward_level(level):
         slot = lax.rem(level, 2)
         m = level + 1
@@ -232,6 +241,11 @@
             each(0, 4, chunk)
 
         each(0, 2, spread)
+
+        @pl.when(level == 0)
+        def _():
+            each(1, LEV, late)
+            each(0, LEV - 1, prepare)
 
         def finish(h):
             def relay(kk):
@@ -319,23 +333,12 @@
 
     rhs_load(0).wait()
 
-    def split_rhs(level):
-        both = rhs_v[level].astype(F32)
-        rhs_f[level, 0] = both[:8]
-        rhs_f[level, 1] = both[8:]
-
     split_rhs(0)
     dinv_load(0).wait()
     each(0, 2, lambda h: solve_forward(0, h, rhs_f[0, h].astype(BF)))
     pl.semaphore_wait(barrier, 64)
     each(0, 2, lambda h: gather_start(0, h))
 
-    def late(level):
-        rhs_load(level).wait()
-        split_rhs(level)
-
-    each(1, LEV, late)
-    each(0, LEV - 1, prepare)
     each(0, LEV - 1, forward_level)
 
     def take_plane(level, h):

time: 126 us -> 126 us (level)
  no operation moved by 1% of the time
where the time goes in v6:
time: 126 us
  Pallas kernels  125 us (99%)
    pallas_call x1, Pallas kernels, shards(): pl.pallas_call(kernel, out_shape=[jax.ShapeDtypeStruct((LEV, H, W), BF)]...  123 us

profile of v6, /device:TPU:1, one launch (start us, length us, event | category | flops | bytes accessed | tf_op | source)
XLA Modules:
  0.0 126.1 jit_solution(12464830901989826138)
XLA Ops:
  0.6 123.1 %levels.1 = (bf16[4,256,512]{2,1,0:T(8,128)(2,1)}, bf16[4,256,512]{2,1,0:T(8,128)(2,1)}) custom-call(bf16[4,1,256,512]{3,2,1,0:T(8,128)(2,1)} %rhs_ref.1, bf16[4,1,512,512]{3,2,1,0:T(8,128)(2,1)} %dinv_ref.1, bf16[3,1,12,512,512]{4,3,2,1,0:T(8,128)(2,1)} %factor_ref.1, s32[3,1,12]{2,1,0:T(1,128)} %deps_ref.1, s32[1,1,3]{2,1,0:T(1,128)} %bitcast.8, ...), custom_call_target="tpu_custom_call" | custom-call | tf_op jit(solution)/shard_map/levels/pallas_call | solution.py:507
  123.7 2.4 %results.1 = (bf16[4,256,512]{2,1,0:T(8,128)(2,1)}, bf16[4,256,512]{2,1,0:T(8,128)(2,1)}) custom-call(bf16[4,256,512]{2,1,0:T(8,128)(2,1)} %get-tuple-element.6.a_in, bf16[4,256,512]{2,1,0:T(8,128)(2,1)} %get-tuple-element.7.b_in), custom_call_target="tpu_custom_call" | custom-call | tf_op jit(solution)/shard_map/results/pallas_call | solution.py:491
